TPU v7x, 256 devices: a whole 4x4x8 slice. The times are simulated.
256 devices in a mesh: row: 16 (over z, x_hi), col: 16 (over y, x_lo, core).
Axes of the slice: x: 4 (x_hi: 2, x_lo: 2; x = x_hi * 2 + x_lo), y: 4, z: 8, core: 2. Of those that a mesh axis runs over, the one named last changes fastest.
Arguments:
- image_features: bfloat16 [8192, 1152], P(('row', 'col')), may hold values from -6 to 6
- text_features: bfloat16 [8192, 1152], P(('col', 'row')), may hold values from -6 to 6
- image_weight: bfloat16 [1152, 1152], replicated, may hold values from -0.1875 to 0.1875
- text_weight: bfloat16 [1152, 1152], replicated, may hold values from -0.1875 to 0.1875
- log_scale: float32 [1], replicated, may hold values from 2.3 to 3.4
- bias: float32 [1], replicated, may hold values from -4 to -2
Outputs:
- image_grad: float32 [8192, 1152], P(('row', 'col'))
- text_grad: float32 [8192, 1152], P(('col', 'row'))
- image_weight_grad: float32 [1152, 1152], P('row')
- text_weight_grad: float32 [1152, 1152], P('row')
All inputs are finite; a program needn't handle non-finite values.
Results may differ from a plain program's by a relative error of at most 0.025.
Values may be sent and summed in bfloat16 or wider, within the bound.
A program may use at most 128 MiB of HBM per device.

v0:
```python
import jax
import jax.numpy as jnp
from jax import lax
from jax.sharding import PartitionSpec as P


def embed_rows(features, weight):
    projected = jnp.dot(features, weight, preferred_element_type=jnp.float32)
    length = jnp.sqrt(jnp.sum(projected * projected, axis=1, keepdims=True) + 1e-06)
    return (length, projected / length)


def unembed_rows(grad_unit, direction, length, weight):
    grad_projected = (
        grad_unit - direction * jnp.sum(direction * grad_unit, axis=1, keepdims=True)
    ) / length
    grad_half = grad_projected.astype(jnp.bfloat16)
    grad_features = lax.dot_general(
        grad_half, weight, (((1,), (1,)), ((), ())), preferred_element_type=jnp.float32
    )
    return (grad_features, grad_half)


def outer_term(features, grad_half):
    return lax.dot_general(
        features, grad_half, (((0,), (0,)), ((), ())), preferred_element_type=jnp.float32
    )


def pair_weights(image_half, text_half, image_start, text_start, log_scale, bias):
    scores = lax.dot_general(
        image_half, text_half, (((1,), (1,)), ((), ())), preferred_element_type=jnp.float32
    )
    factor = jnp.exp(log_scale[0])
    logits = factor * scores + bias[0]
    image_index = image_start + lax.broadcasted_iota(jnp.int32, scores.shape, 0)
    text_index = text_start + lax.broadcasted_iota(jnp.int32, scores.shape, 1)
    labels = jnp.where(image_index == text_index, 1.0, -1.0).astype(jnp.float32)
    return (factor * (-labels * jax.nn.sigmoid(-labels * logits))).astype(jnp.bfloat16)


def body(image_features, text_features, image_weight, text_weight, log_scale, bias):
    image_length, image_dir = embed_rows(image_features, image_weight)
    text_length, text_dir = embed_rows(text_features, text_weight)
    image_half = image_dir.astype(jnp.bfloat16)
    text_half = text_dir.astype(jnp.bfloat16)
    image_block = lax.all_gather(image_half, "col", axis=0, tiled=True)
    text_block = lax.all_gather(text_half, "row", axis=0, tiled=True)
    image_start = lax.axis_index("row") * image_block.shape[0]
    text_start = lax.axis_index("col") * text_block.shape[0]
    weights = pair_weights(image_block, text_block, image_start, text_start, log_scale, bias)
    picked = weights
    image_grad_dir = lax.psum_scatter(
        jnp.dot(picked, text_block, preferred_element_type=jnp.float32).astype(jnp.bfloat16),
        "col",
        scatter_dimension=0,
        tiled=True,
    ).astype(jnp.float32)
    picked = weights
    text_grad_dir = lax.psum_scatter(
        lax.dot_general(
            picked, image_block, (((0,), (0,)), ((), ())), preferred_element_type=jnp.float32
        ).astype(jnp.bfloat16),
        "row",
        scatter_dimension=0,
        tiled=True,
    ).astype(jnp.float32)
    image_grad, image_grad_half = unembed_rows(
        image_grad_dir, image_dir, image_length, image_weight
    )
    text_grad, text_grad_half = unembed_rows(text_grad_dir, text_dir, text_length, text_weight)
    image_term_weight = outer_term(image_features, image_grad_half)
    text_term_weight = outer_term(text_features, text_grad_half)
    shares = (
        lax.psum_scatter(
            image_term_weight.astype(jnp.bfloat16), "row", scatter_dimension=0, tiled=True
        ).astype(jnp.float32),
        lax.psum_scatter(
            text_term_weight.astype(jnp.bfloat16), "row", scatter_dimension=0, tiled=True
        ).astype(jnp.float32),
    )
    image_total, text_total = (
        lax.psum(shares[0].astype(jnp.bfloat16), "col").astype(jnp.float32),
        lax.psum(shares[1].astype(jnp.bfloat16), "col").astype(jnp.float32),
    )
    return (image_grad, text_grad, image_total, text_total)


def solution(mesh):
    in_specs = (P(("row", "col"), None), P(("col", "row"), None), P(), P(), P(), P())
    out_specs = (P(("row", "col"), None), P(("col", "row"), None), P("row", None), P("row", None))
    return jax.shard_map(body, mesh=mesh, in_specs=in_specs, out_specs=out_specs, check_vma=False)
```

profile of v0, /device:TPU:1, one launch (start us, length us, event | category | flops | bytes accessed | tf_op | source)
XLA Modules:
  0.0 798.2 jit_solution(2803710354864165334)
XLA Ops:
  7.2 0.0 copy-start
  7.2 0.0 copy-start.5
  7.2 0.0 all-gather.3.cloned.1.call-start
  7.2 1.7 copy-done
  8.9 1.6 multiply_reduce_fusion.1
  10.5 0.7 fusion.17
  11.2 0.0 all-gather.3.cloned.1.call-update
  11.2 0.0 all-gather.5.cloned.1.call-start
  11.3 0.0 copy-done.5
  11.3 2.4 multiply_reduce_fusion
  13.8 0.7 fusion.18
  14.5 0.0 all-gather.5.cloned.1.call-update
  14.5 0.0 reduce-scatter.5.cloned.1.call-start
  15.9 35.0 %all-gather.3.cloned.1.call-done = bf16[512,1152]{1,0:T(8,128)(2,1)} async-done(((bf16[32,1152]{1,0:T(8,128)(2,1)}), bf16[512,1152]{1,0:T(8,128)(2,1)}) %all-gather.3.cloned.1.call-update) | async-done | bytes 1179664 | tf_op jit(solution)/shard_map/all_gather | solution.py:47
  50.9 78.8 %all-gather.5.cloned.1.call-done = bf16[512,1152]{1,0:T(8,128)(2,1)} async-done(((bf16[32,1152]{1,0:T(8,128)(2,1)}), bf16[512,1152]{1,0:T(8,128)(2,1)}) %all-gather.5.cloned.1.call-update) | async-done | bytes 1179664 | tf_op jit(solution)/shard_map/all_gather | solution.py:48
  129.7 0.0 copy-start.6
  129.7 2.9 fusion.10
  132.6 0.0 copy-start.8
  132.6 0.8 copy-done.8
  133.4 0.0 copy-done.6
  133.4 1.9 convolution_convert_fusion.3
  135.3 0.0 reduce-scatter.5.cloned.1.call-update
  135.3 0.0 copy-start.4
  135.3 0.0 reduce-scatter.7.cloned.1.call-start
  135.4 3.3 convolution_convert_fusion.2
  138.7 0.0 reduce-scatter.7.cloned.1.call-update
  138.8 0.0 all-reduce.9.cloned.1.call-start
  138.8 58.3 %reduce-scatter.5.cloned.1.call-done = bf16[32,1152]{1,0:T(8,128)(2,1)} async-done(((bf16[512,1152]{1,0:T(8,128)(2,1)}), bf16[32,1152]{1,0:T(8,128)(2,1)}) %reduce-scatter.5.cloned.1.call-update) | async-done | bytes 73744 | tf_op jit(solution)/shard_map/reduce_scatter | solution.py:53
  197.1 1.1 fusion.11
  198.1 203.7 %reduce-scatter.7.cloned.1.call-done = bf16[32,1152]{1,0:T(8,128)(2,1)} async-done(((bf16[512,1152]{1,0:T(8,128)(2,1)}), bf16[32,1152]{1,0:T(8,128)(2,1)}) %reduce-scatter.7.cloned.1.call-update) | async-done | bytes 73744 | tf_op jit(solution)/shard_map/reduce_scatter | solution.py:60
  401.8 0.0 copy-start.3
  401.8 1.1 fusion.14
  403.0 0.0 copy-done.4
  403.0 3.4 fusion
  406.4 0.0 copy-done.3
  406.4 2.6 fusion.1
  408.9 0.0 copy-start.7
  408.9 0.0 copy-start.2
  408.9 0.0 all-reduce.9.cloned.1.call-update
  408.9 0.0 all-reduce.7.cloned.1.call-start
  409.0 0.6 copy-done.7
  409.6 0.6 dynamic-slice
  410.8 251.0 %all-reduce.9.cloned.1.call-done = (bf16[1152,1152]{0,1:T(8,128)(2,1)}, bf16[1152,1152]{0,1:T(8,128)(2,1)}) async-done(((bf16[1152,1152]{0,1:T(8,128)(2,1)}, bf16[1152,1152]{0,1:T(8,128)(2,1)}), (bf16[1152,1152]{0,1:T(8,128)(2,1)}, bf16[1152,1152]{0,1:T(8,128)(2,1)})) %all-reduce.9.cloned.1.call-update) | async-done | bytes 5308432
  661.9 1.9 constant_dynamic-slice_fusion.1
  663.8 1.9 constant_dynamic-slice_fusion
  665.7 0.0 all-reduce.7.cloned.1.call-update
  665.8 0.0 copy-done.2
  665.8 0.0 copy-start.1
  665.8 1.6 fusion.23
  667.4 0.2 copy-done.1
  667.5 1.6 fusion.20
  669.1 118.6 %all-reduce.7.cloned.1.call-done = (bf16[72,1152]{0,1:T(8,128)(2,1)}, bf16[72,1152]{0,1:T(8,128)(2,1)}) async-done(((bf16[72,1152]{0,1:T(8,128)(2,1)}, bf16[72,1152]{0,1:T(8,128)(2,1)}), (bf16[72,1152]{0,1:T(8,128)(2,1)}, bf16[72,1152]{0,1:T(8,128)(2,1)})) %all-reduce.7.cloned.1.call-update) | async-done | bytes 331792 | tf_op jit(solution)/shard_map/psum | solution.py:83
  787.7 1.8 copy.12
  789.5 1.8 copy.13
  (3 shorter events, 0.0 us)
Async XLA Ops:
  7.2 1.8 copy-start
  7.2 4.1 copy-start.5
  7.2 43.7 %all-gather.3.cloned.1.call-start = ((), (), s32[]{:S(2)}) async-start(), calls=%async_computation.2 | async-start | bytes 1253376 | tf_op jit(solution)/shard_map/all_gather | solution.py:47
  11.2 118.5 %all-gather.5.cloned.1.call-start = ((), (), s32[]{:S(2)}) async-start(), calls=%async_computation.3 | async-start | bytes 1253376 | tf_op jit(solution)/shard_map/all_gather | solution.py:48
  14.5 182.6 %reduce-scatter.5.cloned.1.call-start = ((), (), s32[]{:S(2)}) async-start(), calls=%async_computation.4 | async-start | bytes 1253376 | tf_op jit(solution)/shard_map/reduce_scatter | solution.py:53
  129.7 3.7 copy-start.6
  132.6 0.8 copy-start.8
  135.3 267.6 %copy-start.4 = (bf16[32,1152]{1,0:T(8,128)(2,1)S(1)}, bf16[32,1152]{1,0:T(8,128)(2,1)}, u32[]{:S(2)}) copy-start(bf16[32,1152]{1,0:T(8,128)(2,1)} %param.6) | copy-start | bytes 221188
  135.3 266.5 %reduce-scatter.7.cloned.1.call-start = ((), (), s32[]{:S(2)}) async-start(), calls=%async_computation.5 | async-start | bytes 1253376 | tf_op jit(solution)/shard_map/reduce_scatter | solution.py:60
  138.8 523.1 %all-reduce.9.cloned.1.call-start = ((), (), s32[]{:S(2)}) async-start(), calls=%async_computation.7 | async-start | bytes 10616832
  401.8 4.5 copy-start.3
  408.9 0.7 copy-start.7
  408.9 256.8 %copy-start.2 = (bf16[32,1152]{1,0:T(8,128)(2,1)S(1)}, bf16[32,1152]{1,0:T(8,128)(2,1)}, u32[]{:S(2)}) copy-start(bf16[32,1152]{1,0:T(8,128)(2,1)} %reduce-scatter.5.cloned.1.call-done) | copy-start | bytes 221188
  408.9 378.7 %all-reduce.7.cloned.1.call-start = ((), (), s32[]{:S(2)}) async-start(), calls=%async_computation.6 | async-start | bytes 1179648 | tf_op jit(solution)/shard_map/psum | solution.py:83
  665.8 1.8 copy-start.1
Sparse Core Ops, SparseCore 0:
  11.4 39.4 all-gather.2
  54.1 75.5 all-gather.4
  135.4 61.5 reduce-scatter.4
  200.8 200.9 reduce-scatter.6
  409.1 252.7 all-reduce.8
  665.9 121.7 all-reduce.6
where the time goes:
time: 800 us; the launch traced here: 798 us
  waiting for transfers between devices  745 us (93%)
  matrix products  21.2 us (3%)
  between operations  16.2 us (2%)
  local copies, waits for them, and re-layouts  11.4 us (1%)
    unnamed x7, waiting for transfers between devices  251 us
    reduce_scatter x1, waiting for transfers between devices, body(): lax.psum_scatter(lax.dot_general(picked, image_block, (((0,), (0,)), ((),...  204 us
    psum x1, waiting for transfers between devices, body(): lax.psum(shares[0].astype(jnp.bfloat16), 'col').astype(jnp.float32)  119 us
    all_gather x1, waiting for transfers between devices, body(): text_block = lax.all_gather(text_half, 'row', axis=0, tiled=True)  78.8 us
    reduce_scatter x1, waiting for transfers between devices, body(): lax.psum_scatter(jnp.dot(picked, text_block, preferred_element_type=jnp.f...  58.3 us
    all_gather x1, waiting for transfers between devices, body(): image_block = lax.all_gather(image_half, 'col', axis=0, tiled=True)  35 us
  transfers between devices with their start and end apart: 6, of which 6 were waited for; matrix products, arithmetic and copies ran while one was open for 1% of the time, Pallas kernels for 0%

commit v1 on v0

v1 whole, which is shorter than its diff:
```python
import functools

import jax
import jax.numpy as jnp
from jax import lax
from jax.experimental import pallas as pl
from jax.experimental.pallas import tpu as pltpu
from jax.sharding import PartitionSpec as P

MESH = pl.DeviceIdType.MESH
BF = jnp.bfloat16
F32 = jnp.float32
W = 1152
R = 32
B = 512
Q = 128
U = 72
UP = 80
NB = 9


def place():
    r, c = lax.axis_index("row"), lax.axis_index("col")
    return r // 2, c // 4, (r % 2) * 2 + (c % 4) // 2, c % 2


def device(z, y, x, k):
    return (z * 2 + x // 2, y * 4 + (x % 2) * 2 + k)


def push(src, dst, send, recv, to):
    return pltpu.make_async_remote_copy(
        src_ref=src, dst_ref=dst, send_sem=send, recv_sem=recv, device_id=to, device_id_type=MESH
    )


def dot(a, b):
    return jnp.dot(a, b, preferred_element_type=F32)


def dot_nt(a, b):
    return lax.dot_general(a, b, (((1,), (1,)), ((), ())), preferred_element_type=F32)


def dot_tn(a, b):
    return lax.dot_general(a, b, (((0,), (0,)), ((), ())), preferred_element_type=F32)


def each(lo, hi, fn):
    def step(i, carry):
        fn(i)
        return carry

    lax.fori_loop(lo, hi, step, 0)


def kernel(
    xi, xt, wi_hbm, wt_hbm, ls, bs,
    oi, ot, owi, owt,
    WI, WT, XI, XT, HI, HT, PW, XIT, XTT,
    DI, LI, DT, LT,
    ST, CT, GT, S2, RT, SI, RI, GI,
    GB, PI, TB, PT, PARI, PART, SB, CB, UB, UI, VB, UT, CO, FB,
    wsem, ai_s, ai_r, at_s, at_r, ac_s, ac_r, ct_s, ct_r, rt_s, rt_r, ri_s, ri_r,
    pi_s, pi_r, pt_s, pt_r, cb_s, cb_r, ui_s, ui_r, ut_s, ut_r, fb_s, fb_r,
):
    z, y, x, k = place()
    p0 = y * 4 + x
    sib = device(z, y, x, 1 - k)

    def plane_to(i):
        return device(z, (y + i // 4) % 4, (x + i % 4) % 4, k)

    def plane_back(i):
        return device(z, (y + 4 - i // 4) % 4, (x + 4 - i % 4) % 4, k)

    def line_to(d):
        return device((z + d) % 8, y, x, k)

    def line_back(d):
        return device((z + 8 - d) % 8, y, x, k)

    load_i = pltpu.make_async_copy(wi_hbm, WI, wsem.at[0])
    load_t = pltpu.make_async_copy(wt_hbm, WT, wsem.at[1])
    load_i.start()
    load_t.start()

    bar = pltpu.get_barrier_semaphore()
    each(1, 16, lambda i: pl.semaphore_signal(bar, inc=1, device_id=plane_to(i), device_id_type=MESH))
    each(1, 8, lambda d: pl.semaphore_signal(bar, inc=1, device_id=line_to(d), device_id_type=MESH))
    pl.semaphore_signal(bar, inc=1, device_id=sib, device_id_type=MESH)
    pl.semaphore_wait(bar, 23)

    def ai(i):
        return push(xi, XI.at[i], ai_s.at[i], ai_r.at[i], plane_to(i))

    def at(d):
        return push(xt, XT.at[d], at_s.at[d], at_r.at[d], line_to(d))

    def ac(d):
        return push(XT.at[d], XT.at[8 + d], ac_s.at[d], ac_r.at[d], sib)

    XT[0] = xt[...]
    XI[0] = xi[...]
    each(1, 8, lambda d: at(d).start())
    each(1, 16, lambda i: ai(i).start())
    ac(0).start()

    def forward(d):
        at(d).wait_recv()
        ac(d).start()

    def project(c, X, WW, H, D, L):
        p = dot(X[pl.ds(c * 4, 4)].reshape(Q, W), WW[...])
        length = jnp.sqrt(jnp.sum(p * p, axis=1, keepdims=True) + 1e-06)
        p = p / length
        H[pl.ds(pl.multiple_of(c * Q, Q), Q)] = p.astype(BF)

        @pl.when(c == 0)
        def _():
            D[...] = p[:R]
            L[...] = length[:R]

    forward(1)
    forward(7)
    forward(2)
    forward(6)
    load_i.wait()

    def image_chunk(c):
        def arrive(i):
            @pl.when(i > 0)
            def _():
                ai(i).wait_recv()

        each(c * 4, c * 4 + 4, arrive)
        project(c, XI, WI, HI, DI, LI)

    each(0, 2, image_chunk)
    forward(3)
    forward(5)
    each(2, 4, image_chunk)
    forward(4)
    load_t.wait()

    def text_chunk(c):
        def arrive(s):
            @pl.when(s >= 8)
            def _():
                ac(s - 8).wait_recv()

        each(c * 4, c * 4 + 4, arrive)
        project(c, XT, WT, HT, DT, LT)

    each(0, 4, text_chunk)

    factor = jnp.exp(ls[...])
    bias = bs[...]
    col = lax.broadcasted_iota(jnp.int32, (1, B), 1)
    cs = col >> 5
    cz = (z - (cs & 7)) & 7
    ck = k ^ (cs >> 3)
    tid = (y * 4 + (x % 2) * 2 + ck) * B + (cz * 2 + x // 2) * R + (col & 31)

    def pair_chunk(c):
        row = lax.broadcasted_iota(jnp.int32, (Q, 1), 0) + c * Q
        rs = row >> 5
        ry = (y - (rs >> 2)) & 3
        rx = (x - (rs & 3)) & 3
        iid = (z * 2 + (rx >> 1)) * B + (ry * 4 + ((rx & 1) << 1) + k) * R + (row & 31)
        rows = pl.ds(pl.multiple_of(c * Q, Q), Q)
        logits = factor * dot_nt(HI[rows], HT[...]) + bias
        same = iid == tid
        signed = jnp.where(same, -logits, logits)
        weight = factor / (1.0 + jnp.exp(-signed))
        PW[rows] = jnp.where(same, -weight, weight).astype(BF)

    each(0, 4, pair_chunk)

    def ct(c):
        half = pl.ds(c * 4, 4)
        return push(ST.at[half], CT.at[half], ct_s.at[c], ct_r.at[c], sib)

    def text_grad(c):
        g = dot_tn(PW[:, pl.ds(pl.multiple_of(c * Q, Q), Q)], HI[...])

        @pl.when(c >= 2)
        def _():
            ST[pl.ds((c - 2) * 4, 4)] = g.astype(BF).reshape(4, R, W)
            ct(c - 2).start()

        @pl.when(c < 2)
        def _():
            GT[pl.ds(c * 4, 4)] = g.reshape(4, R, W)

    each(2, 4, text_grad)
    each(0, 2, text_grad)

    def rt(d):
        return push(S2.at[d], RT.at[d], rt_s.at[d], rt_r.at[d], line_back(d))

    def text_send(d):
        @pl.when(d % 4 == 0)
        def _():
            ct(d // 4).wait_recv()

        @pl.when(d > 0)
        def _():
            S2[d] = (GT[d] + CT[d].astype(F32)).astype(BF)
            rt(d).start()

    each(0, 8, text_send)

    def ri(i):
        return push(SI.at[i], RI.at[i], ri_s.at[i], ri_r.at[i], plane_back(i))

    def image_grad(c):
        g = dot(PW[pl.ds(pl.multiple_of(c * Q, Q), Q)], HT[...])
        SI[pl.ds(c * 4, 4)] = g.astype(BF).reshape(4, R, W)

        @pl.when(c == 0)
        def _():
            GI[...] = g[:R]

        def send(i):
            @pl.when(i > 0)
            def _():
                ri(i).start()

        each(c * 4, c * 4 + 4, send)

    each(0, 4, image_grad)

    def flip(j):
        lanes = pl.ds(pl.multiple_of(j * Q, Q), Q)
        XIT[lanes] = XI[:, :, lanes].reshape(B, Q).T
        XTT[lanes] = XT[:, :, lanes].reshape(B, Q).T

    each(0, NB, flip)

    def unembed(g, D, L, blocks):
        d = D[...]
        half = ((g - d * jnp.sum(d * g, axis=1, keepdims=True)) / L[...]).astype(BF)
        for j in range(NB):
            blocks[j] = half[:, j * Q : (j + 1) * Q]
        return half

    def image_sum(i, acc):
        ri(i).wait_recv()
        return acc + RI[i].astype(F32)

    half_i = unembed(lax.fori_loop(1, 16, image_sum, GI[...]), DI, LI, GB)

    def plane_index(i):
        return ((y + i // 4) % 4) * 4 + (x + i % 4) % 4

    def pi(i):
        return push(GB.at[plane_index(i)], PI.at[i], pi_s.at[i], pi_r.at[i], plane_to(i))

    def pi_send(i):
        @pl.when(plane_index(i) < NB)
        def _():
            pi(i).start()

    each(1, 16, pi_send)
    active = p0 < NB

    oi[...] = dot_nt(half_i, WI[...])

    def cb():
        return push(SB, CB, cb_s.at[0], cb_r.at[0], sib)

    def ui(d):
        return push(UB.at[d], UI.at[d], ui_s.at[d], ui_r.at[d], line_to(d))

    def head_rows(zz, h):
        return pl.ds(pl.multiple_of(zz * (2 * U) + h * U, 8), U)

    @pl.when(active)
    def _():
        PI[0] = GB[p0]

        def arrive(i):
            push(GB.at[0], PI.at[i], pi_s.at[i], pi_r.at[i], plane_to(i)).wait_recv()

        each(1, 16, arrive)
        PARI[...] = dot(XIT[...], PI[...].reshape(B, Q))

        def give(d):
            SB[d, 0:U] = PARI[head_rows((z + d) % 8, 1 - k)].astype(BF)
            SB[d, U:UP] = jnp.zeros((UP - U, Q), BF)

        each(0, 8, give)
        cb().start()
        cb().wait_recv()

        def pass_on(d):
            UB[d, 0:U] = (PARI[head_rows((z + d) % 8, k)] + CB[d, 0:U].astype(F32)).astype(BF)
            UB[d, U:UP] = jnp.zeros((UP - U, Q), BF)

            @pl.when(d > 0)
            def _():
                ui(d).start()

        each(0, 8, pass_on)

    def text_sum(d, acc):
        rt(d).wait_recv()
        return acc + RT[d].astype(F32)

    half_t = unembed(lax.fori_loop(1, 8, text_sum, GT[0] + CT[0].astype(F32)), DT, LT, TB)

    def pt(s):
        zz = (z + s % 8) % 8
        kk = (k + s // 8) % 2
        block = jnp.where(kk == 0, zz, 8)
        return push(TB.at[block], PT.at[s], pt_s.at[s], pt_r.at[s], device(zz, y, x, kk))

    each(1, 16, lambda s: pt(s).start())
    PT[0] = TB[jnp.where(k == 0, z, 8)]
    ot[...] = dot_nt(half_t, WT[...])
    each(1, 16, lambda s: pt(s).wait_recv())
    PART[...] = dot(XTT[...], PT[...].reshape(B, Q))

    mine = jnp.where(k == 0, z, 8)

    def ut(u):
        to = device(u // 2, mine // 4, mine % 4, u % 2)
        return push(VB.at[u], UT.at[p0], ut_s.at[u], ut_r.at[p0], to)

    def ut_here(u):
        return (u // 2 == z) & (mine == p0) & (u % 2 == k)

    def ut_used(u):
        return (k == 0) | (u // 2 == z)

    def ut_send(u):
        @pl.when(ut_used(u))
        def _():
            VB[u, 0:U] = PART[pl.ds(pl.multiple_of(u * U, 8), U)].astype(BF)
            VB[u, U:UP] = jnp.zeros((UP - U, Q), BF)

            @pl.when(ut_here(u))
            def _():
                UT[p0] = VB[u]

            @pl.when(jnp.logical_not(ut_here(u)))
            def _():
                ut(u).start()

    each(0, 16, ut_send)

    def fb(t):
        to = device(z, t // 4, k * 2 + (t // 2) % 2, t % 2)
        return push(CO, FB.at[p0], fb_s.at[t], fb_r.at[p0], to)

    def fb_here(t):
        return (t // 4 == y) & (k * 2 + (t // 2) % 2 == x) & (t % 2 == k)

    @pl.when(active)
    def _():
        def add_image(d, acc):
            ui(d).wait_recv()
            return acc + UI[d, 0:U].astype(F32)

        image = lax.fori_loop(1, 8, add_image, UB[0, 0:U].astype(F32))
        own = jnp.where(p0 < 8, (z == p0) & (k == 0), k == 1)

        def add_text(q, acc):
            @pl.when(jnp.logical_not(own & (q == p0)))
            def _():
                push(VB.at[0], UT.at[q], ut_s.at[0], ut_r.at[q], sib).wait_recv()

            return acc + UT[q, 0:U].astype(F32)

        text = lax.fori_loop(0, 16, add_text, jnp.zeros((U, Q), F32))
        CO[...] = jnp.concatenate([image, text], axis=0).astype(BF)

        def send(t):
            @pl.when(fb_here(t))
            def _():
                FB[p0] = CO[...]

            @pl.when(jnp.logical_not(fb_here(t)))
            def _():
                fb(t).start()

        each(0, 16, send)

    for j in range(NB):

        @pl.when(jnp.logical_not((p0 == j) & (x // 2 == k)))
        def _():
            push(CO, FB.at[j], fb_s.at[0], fb_r.at[j], sib).wait_recv()

        both = FB[j].astype(F32)
        owi[:, j * Q : (j + 1) * Q] = both[:U]
        owt[:, j * Q : (j + 1) * Q] = both[U:]

    each(1, 16, lambda i: ai(i).wait_send())
    each(1, 8, lambda d: at(d).wait_send())
    each(0, 8, lambda d: ac(d).wait_send())
    each(0, 2, lambda c: ct(c).wait_send())
    each(1, 8, lambda d: rt(d).wait_send())
    each(1, 16, lambda i: ri(i).wait_send())

    def pi_sent(i):
        @pl.when(plane_index(i) < NB)
        def _():
            pi(i).wait_send()

    each(1, 16, pi_sent)
    each(1, 16, lambda s: pt(s).wait_send())

    def ut_sent(u):
        @pl.when(ut_used(u) & jnp.logical_not(ut_here(u)))
        def _():
            ut(u).wait_send()

    each(0, 16, ut_sent)

    @pl.when(active)
    def _():
        cb().wait_send()
        each(1, 8, lambda d: ui(d).wait_send())

        def fb_sent(t):
            @pl.when(jnp.logical_not(fb_here(t)))
            def _():
                fb(t).wait_send()

        each(0, 16, fb_sent)


def body(image_features, text_features, image_weight, text_weight, log_scale, bias):
    vmem = pl.BlockSpec(memory_space=pltpu.VMEM)
    hbm = pl.BlockSpec(memory_space=pl.ANY)
    v = pltpu.VMEM
    dma = pltpu.SemaphoreType.DMA
    return pl.pallas_call(
        kernel,
        out_shape=(
            jax.ShapeDtypeStruct((R, W), F32),
            jax.ShapeDtypeStruct((R, W), F32),
            jax.ShapeDtypeStruct((U, W), F32),
            jax.ShapeDtypeStruct((U, W), F32),
        ),
        in_specs=[vmem, vmem, hbm, hbm, vmem, vmem],
        out_specs=(vmem, vmem, vmem, vmem),
        scratch_shapes=[
            v((W, W), BF), v((W, W), BF), v((16, R, W), BF), v((16, R, W), BF), v((B, W), BF), v((B, W), BF), v((B, B), BF),
            v((W, B), BF), v((W, B), BF),
            v((R, W), F32), v((R, 1), F32), v((R, W), F32), v((R, 1), F32),
            v((8, R, W), BF), v((8, R, W), BF), v((8, R, W), F32), v((8, R, W), BF), v((8, R, W), BF),
            v((16, R, W), BF), v((16, R, W), BF), v((R, W), F32),
            v((NB, R, Q), BF), v((16, R, Q), BF), v((NB, R, Q), BF), v((16, R, Q), BF), v((W, Q), F32), v((W, Q), F32),
            v((8, UP, Q), BF), v((8, UP, Q), BF), v((8, UP, Q), BF), v((8, UP, Q), BF), v((16, UP, Q), BF), v((16, UP, Q), BF),
            v((2 * U, Q), BF), v((NB, 2 * U, Q), BF),
            dma((2,)), dma((16,)), dma((16,)), dma((8,)), dma((8,)), dma((8,)), dma((8,)), dma((2,)), dma((2,)), dma((8,)), dma((8,)),
            dma((16,)), dma((16,)), dma((16,)), dma((16,)), dma((16,)), dma((16,)), dma((1,)), dma((1,)), dma((8,)), dma((8,)),
            dma((16,)), dma((16,)), dma((16,)), dma((NB,)),
        ],
        compiler_params=pltpu.CompilerParams(
            collective_id=0, has_side_effects=True, vmem_limit_bytes=50 * 1024 * 1024
        ),
    )(
        image_features, text_features, image_weight, text_weight,
        log_scale.reshape(1, 1), bias.reshape(1, 1),
    )


def solution(mesh):
    in_specs = (P(("row", "col"), None), P(("col", "row"), None), P(), P(), P(), P())
    out_specs = (P(("row", "col"), None), P(("col", "row"), None), P("row", None), P("row", None))
    return jax.shard_map(body, mesh=mesh, in_specs=in_specs, out_specs=out_specs, check_vma=False)
```

time: 800 us -> 103 us (0.13)
  the two profiles are of different devices: /device:TPU:1 before, /device:TPU:25 now
where the time goes in v1:
time: 103 us
  Pallas kernels  94.3 us (92%)
  local copies, waits for them, and re-layouts  6.28 us (6%)
  between operations  1.94 us (2%)
    pallas_call x1, Pallas kernels, body(): pl.pallas_call(kernel, out_shape=(jax.ShapeDtypeStruct((R, W), F32), jax....  94.3 us
    unnamed x10, local copies, waits for them, and re-layouts  6.28 us

profile of v1, /device:TPU:25, one launch (start us, length us, event | category | flops | bytes accessed | tf_op | source)
XLA Modules:
  0.0 102.5 jit_solution(11657726844942319346)
XLA Ops:
  1.9 0.0 copy-start
  1.9 1.7 %copy-done = bf16[1152,1152]{1,0:T(8,128)(2,1)S(1)} copy-done((bf16[1152,1152]{1,0:T(8,128)(2,1)S(1)}, bf16[1152,1152]{1,0:T(8,128)(2,1)}, u32[]{:S(2)}) %copy-start) | copy-done | bytes 2654232
  3.7 0.0 copy-start.1
  3.7 0.9 copy-done.1
  4.6 0.0 copy-start.2
  4.6 0.9 copy-done.2
  5.4 94.3 %shard_map.93 = (f32[32,1152]{1,0:T(8,128)S(1)}, f32[32,1152]{1,0:T(8,128)S(1)}, f32[72,1152]{1,0:T(8,128)S(1)}, f32[72,1152]{1,0:T(8,128)S(1)}) custom-call(bf16[32,1152]{1,0:T(8,128)(2,1)S(1)} %copy-done.1, bf16[32,1152]{1,0:T(8,128)(2,1)S(1)} %copy-done.2, bf16[1152,1152]{1,0:T(8,128)(2,1)S(1)} %copy-done, bf16[1152,1152]{1,0:T(8,128)(2,1)} %wt_hbm.1, ...), custom_call_target="tpu_custom_call" | custom-call | tf_op jit(solution)/shard_map/pallas_call | solution.py:440
  99.7 0.7 copy.16
  100.4 0.7 copy.17
  101.1 0.7 copy.18
  101.8 0.7 copy.19
Async XLA Ops:
  1.9 1.8 %copy-start = (bf16[1152,1152]{1,0:T(8,128)(2,1)S(1)}, bf16[1152,1152]{1,0:T(8,128)(2,1)}, u32[]{:S(2)}) copy-start(bf16[1152,1152]{1,0:T(8,128)(2,1)} %wi_hbm.1) | copy-start | bytes 7962628
  3.7 0.9 copy-start.1
  4.6 0.9 copy-start.2

commit v2 on v0

v2 whole, which is shorter than its diff:
```python
import jax
import jax.numpy as jnp
from jax import lax
from jax.experimental import pallas as pl
from jax.experimental.pallas import tpu as pltpu
from jax.sharding import PartitionSpec as P

MESH = pl.DeviceIdType.MESH
BF = jnp.bfloat16
F32 = jnp.float32
W = 1152
R = 32
H = 16
B = 512
Q = 128
U = 72
UP = 80
NB = 9
TEXT_AT = 7
ORDER = (0, 1, 7, 2, 6, 3, 5, 4)
POS = {d: n for n, d in enumerate(ORDER)}


def place():
    r, c = lax.axis_index("row"), lax.axis_index("col")
    return r // 2, c // 4, (r % 2) * 2 + (c % 4) // 2, c % 2


def other(s):
    return 8 + (s + 4) % 8


def device(z, y, x, k):
    return (z * 2 + x // 2, y * 4 + (x % 2) * 2 + k)


def push(src, dst, send, recv, to):
    return pltpu.make_async_remote_copy(
        src_ref=src, dst_ref=dst, send_sem=send, recv_sem=recv, device_id=to, device_id_type=MESH
    )


def dot(a, b):
    return jnp.dot(a, b, preferred_element_type=F32)


def dot_nt(a, b):
    return lax.dot_general(a, b, (((1,), (1,)), ((), ())), preferred_element_type=F32)


def dot_tn(a, b):
    return lax.dot_general(a, b, (((0,), (0,)), ((), ())), preferred_element_type=F32)


def each(lo, hi, fn):
    def step(i, carry):
        fn(i)
        return carry

    lax.fori_loop(lo, hi, step, 0)


def kernel(
    both_x, wi_hbm, wt_hbm, ls, bs,
    out,
    WI, WT, XI, XT, HI, HT, PW, XIT, XTT,
    DI, LI, DT, LT,
    ST, CT, GT, S2, RA, RB, RM, RT, SI, R1, R2, N1, N2, F1, F2,
    GB, PI, TB, PT, PARI, PART, SB, CB, UB, UI, VB, UT, CI, CX, FI, FT,
    lsem, at_s, at_r, ac_s, ac_r, ax_s, ax_r, ay_s, ay_r, a1_s, a1_r, a2_s, a2_r,
    ct_s, ct_r, ra_s, ra_r, rb_s, rb_r, rt_s, rt_r, r1_s, r1_r, r2_s, r2_r, f1_s, f1_r, f2_s, f2_r,
    pi_s, pi_r, pt_s, pt_r, cb_s, cb_r, ui_s, ui_r, ut_s, ut_r, fi_s, fi_r, ft_s, ft_r,
):
    z, y, x, k = place()
    p0 = y * 4 + x
    sib = device(z, y, x, 1 - k)

    def at_z(d):
        return device((z + d + 8) % 8, y, x, k)

    def at_y(d):
        return device(z, (y + d + 4) % 4, x, k)

    def at_x(d):
        return device(z, y, (x + d + 4) % 4, k)

    loads = [
        pltpu.make_async_copy(src, dst, lsem.at[n])
        for n, (src, dst) in enumerate(((both_x.at[1], XT.at[0]), (both_x.at[0], XI.at[0, 0]), (wt_hbm, WT), (wi_hbm, WI)))
    ]
    for load in loads:
        load.start()

    bar = pltpu.get_barrier_semaphore()
    near = [at_z(d) for d in (1, -1, 2, -2)] + [at_x(d) for d in (1, 2, 3)] + [at_y(d) for d in (1, 2, 3)] + [sib]
    for to in near:
        pl.semaphore_signal(bar, inc=1, device_id=to, device_id_type=MESH)

    pad = jnp.zeros((8, UP - U, Q), BF)
    for buf in (SB, UB, VB.at[0:8], VB.at[8:16]):
        buf[:, U:UP] = pad
    CI[U:UP] = pad[0]
    CX[U:UP] = pad[0]

    loads[0].wait()
    loads[1].wait()
    pl.semaphore_wait(bar, len(near))

    def tz(d, d_to, n, rows=None):
        src, dst = XT.at[POS[d % 8]], XT.at[POS[(d + d_to) % 8]]
        if rows is not None:
            src, dst = src.at[pl.ds(rows, H)], dst.at[pl.ds(rows, H)]
        return push(src, dst, at_s.at[n], at_r.at[n], at_z(d_to))

    z_near = {1: tz(0, 1, 0), 7: tz(0, -1, 1), 2: tz(0, 2, 2), 6: tz(0, -2, 3)}
    z_far = {3: tz(2, 1, 4), 5: tz(-2, -1, 5), 4: tz(2, 2, 6, 0), 12: tz(-2, -2, 7, H)}

    def ac(s):
        return push(XT.at[s], XT.at[other(s)], ac_s.at[s], ac_r.at[s], sib)

    def ax(d):
        return push(XI.at[0, 0], XI.at[0, d], ax_s.at[d], ax_r.at[d], at_x(d))

    def ay(d):
        return push(XI.at[0, 0], XI.at[d, 0], ay_s.at[d], ay_r.at[d], at_y(d))

    def a1(d):
        rows = pl.ds(0, H)
        return push(XI.at[0, 1:4, rows], XI.at[d, 1:4, rows], a1_s.at[d], a1_r.at[d], at_y(d))

    def a2(d):
        rows = pl.ds(H, H)
        return push(XI.at[1:4, 0, rows], XI.at[1:4, d, rows], a2_s.at[d], a2_r.at[d], at_x(d))

    z_near[2].start()
    z_near[6].start()
    for d in (2, 1, 3):
        ax(d).start()
        ay(d).start()
    z_near[1].start()
    z_near[7].start()
    ac(0).start()

    def project(x_in, n, WW, HH, c):
        p = dot(x_in.reshape(n * Q, W), WW[...])
        length = jnp.sqrt(jnp.sum(p * p, axis=1, keepdims=True) + 1e-06)
        p = p * (1.0 / length)
        HH[c * Q : (c + n) * Q] = p.astype(BF)
        return p, length

    def arrived(copies):
        for copy in copies:
            copy.wait_recv()

    def relay():
        z_near[2].wait_recv()
        z_far[4].start()
        z_far[3].start()
        ac(POS[2]).start()
        z_near[6].wait_recv()
        z_far[12].start()
        z_far[5].start()
        ac(POS[6]).start()
        for d in (1, 7):
            z_near[d].wait_recv()
            ac(POS[d]).start()

    relay()
    arrived(ax(d) for d in (1, 3, 2))
    for d in (2, 1, 3):
        a1(d).start()
    arrived(ay(d) for d in (1, 3, 2))
    for d in (2, 1, 3):
        a2(d).start()

    loads[2].wait()
    p, length = project(XT[0:4], 1, WT, HT, 0)
    DT[...] = p[:R]
    LT[...] = length[:R]
    loads[3].wait()
    p, length = project(XI[0], 1, WI, HI, 0)
    DI[...] = p[:R]
    LI[...] = length[:R]

    arrived([z_far[3]])
    ac(POS[3]).start()
    arrived([z_far[5]])
    ac(POS[5]).start()
    arrived([z_far[4], z_far[12]])
    ac(POS[4]).start()
    arrived(ac(s) for s in range(4))
    project(XT[12:16], 1, WT, HT, 3)
    arrived(a2(d) for d in (1, 2, 3))
    arrived(a1(d) for d in (1, 3, 2))
    project(XI[1:4], 3, WI, HI, 1)
    arrived(ac(s) for s in range(4, 8))
    project(XT[4:12], 2, WT, HT, 1)

    factor = jnp.exp(ls[...])
    bias = bs[...]
    col = lax.broadcasted_iota(jnp.int32, (1, B), 1)
    cs = col >> 5
    cd = jnp.zeros_like(cs)
    for n, d in enumerate(ORDER):
        cd = jnp.where((cs == n) | (cs == other(n)), d, cd)
    cz = (z - cd) & 7
    ck = k ^ (cs >> 3)
    tid = (y * 4 + (x % 2) * 2 + ck) * B + (cz * 2 + x // 2) * R + (col & 31)
    row = lax.broadcasted_iota(jnp.int32, (B, 1), 0)
    rs = row >> 5
    ry = (y - (rs >> 2)) & 3
    rx = (x - (rs & 3)) & 3
    iid = (z * 2 + (rx >> 1)) * B + (ry * 4 + ((rx & 1) << 1) + k) * R + (row & 31)

    def pair(c, n):
        cols = slice(c * Q, (c + n) * Q)
        logits = factor * dot_nt(HI[...], HT[cols]) + bias
        same = iid == tid[:, cols]
        signed = jnp.where(same, -logits, logits)
        weight = factor / (1.0 + jnp.exp(-signed))
        PW[:, cols] = jnp.where(same, -weight, weight).astype(BF)

    def text_grad(c):
        return dot_tn(PW[:, c * Q : (c + 1) * Q], HI[...]).reshape(4, R, W)

    def ct(c):
        half = pl.ds(c * 4, 4)
        return push(ST.at[half], CT.at[half], ct_s.at[c], ct_r.at[c], sib)

    near_t = {1: push(S2.at[0], RT.at[0], rt_s.at[0], rt_r.at[0], at_z(-1)),
              7: push(S2.at[1], RT.at[1], rt_s.at[1], rt_r.at[1], at_z(1))}
    relay_t = {3: push(S2.at[2], RA.at[0], ra_s.at[0], ra_r.at[0], at_z(-1)),
               5: push(S2.at[3], RA.at[1], ra_s.at[1], ra_r.at[1], at_z(1))}
    half_t = [push(S2.at[4, pl.ds(n * H, H)], RB.at[n], rb_s.at[n], rb_r.at[n], at_z(2 * (2 * n - 1))) for n in (0, 1)]
    sum_t = [push(RM.at[n], RT.at[2 + n], rt_s.at[2 + n], rt_r.at[2 + n], at_z(2 * (2 * n - 1))) for n in (0, 1)]

    def both(d):
        return GT[POS[d]] + CT[POS[d]].astype(F32)

    pair(1, 2)
    ST[4:8] = text_grad(2).astype(BF)
    ct(1).start()
    GT[4:8] = text_grad(1)
    pair(0, 1)
    pair(3, 1)
    ct(1).wait_recv()
    S2[4] = both(4).astype(BF)
    half_t[0].start()
    half_t[1].start()
    S2[2] = both(3).astype(BF)
    relay_t[3].start()
    S2[3] = both(5).astype(BF)
    relay_t[5].start()
    ST[0:4] = text_grad(3).astype(BF)
    ct(0).start()

    def r1(d):
        return push(SI.at[d, :, pl.ds(0, H)], R1.at[d], r1_s.at[d], r1_r.at[d], at_y(-d))

    def r2(d):
        return push(SI.at[:, d, pl.ds(H, H)], R2.at[d], r2_s.at[d], r2_r.at[d], at_x(-d))

    for c in (2, 1, 3, 0):
        SI[c] = dot(PW[c * Q : (c + 1) * Q], HT[...]).astype(BF).reshape(4, R, W)
        if c > 0:
            r1(c).start()
    for d in (2, 1, 3):
        r2(d).start()

    GT[0:4] = text_grad(0)
    ct(0).wait_recv()
    S2[0] = both(1).astype(BF)
    near_t[1].start()
    S2[1] = both(7).astype(BF)
    near_t[7].start()

    for n, (d_near, d_far) in enumerate(((2, 3), (6, 5))):
        relay_t[d_far].wait_recv()
        half_t[n].wait_recv()
        m = both(d_near) + RA[n].astype(F32)
        extra = RB[n].astype(F32)
        rows, rest = (slice(0, H), slice(H, R)) if n == 0 else (slice(H, R), slice(0, H))
        RM[n, rows] = (m[rows] + extra).astype(BF)
        RM[n, rest] = m[rest].astype(BF)
        sum_t[n].start()

    def flip(j):
        lanes = pl.ds(pl.multiple_of(j * Q, Q), Q)
        XIT[lanes] = XI[:, :, :, lanes].reshape(B, Q).T
        XTT[lanes] = XT[:, :, lanes].reshape(B, Q).T

    each(0, NB, flip)

    def f1(d):
        return push(N1.at[d], F1.at[d], f1_s.at[d], f1_r.at[d], at_x(-d))

    def f2(d):
        return push(N2.at[d], F2.at[d], f2_s.at[d], f2_r.at[d], at_y(-d))

    arrived(r1(d) for d in (1, 3, 2))

    def sum1(d):
        N1[d] = (SI[0, d, 0:H].astype(F32) + R1[1, d].astype(F32) + R1[2, d].astype(F32) + R1[3, d].astype(F32)).astype(BF)

    def sum2(d):
        N2[d] = (SI[d, 0, H:R].astype(F32) + R2[1, d].astype(F32) + R2[2, d].astype(F32) + R2[3, d].astype(F32)).astype(BF)

    for d in (2, 1, 3):
        sum1(d)
        f1(d).start()
    sum1(0)
    arrived(r2(d) for d in (1, 3, 2))
    for d in (2, 1, 3):
        sum2(d)
        f2(d).start()
    sum2(0)

    def unembed(g, D, L, blocks):
        d = D[...]
        half = ((g - d * jnp.sum(d * g, axis=1, keepdims=True)) / L[...]).astype(BF)
        for j in range(NB):
            blocks[j] = half[:, j * Q : (j + 1) * Q]
        return half

    arrived((near_t[1], near_t[7], sum_t[0], sum_t[1]))
    g = both(0)
    for n in range(4):
        g = g + RT[n].astype(F32)
    half_text = unembed(g, DT, LT, TB)
    mine = jnp.where(k == 0, z, 8)

    def pt(s):
        zz = (z + s % 8) % 8
        kk = (k + s // 8) % 2
        slot = POS[s % 8] if s < 8 else other(POS[s % 8])
        return push(TB.at[jnp.where(kk == 0, zz, 8)], PT.at[slot], pt_s.at[s], pt_r.at[s], device(zz, y, x, kk))

    for s in range(1, 16):
        pt(s).start()
    PT[0] = TB[mine]

    arrived(f1(d) for d in (1, 3, 2))
    arrived(f2(d) for d in (1, 3, 2))
    g1 = N1[0].astype(F32)
    g2 = N2[0].astype(F32)
    for d in (1, 2, 3):
        g1 = g1 + F1[d].astype(F32)
        g2 = g2 + F2[d].astype(F32)
    half_image = unembed(jnp.concatenate([g1, g2], axis=0), DI, LI, GB)

    def plane_index(i):
        return ((y + i // 4) % 4) * 4 + (x + i % 4) % 4

    def pi(i, block=None):
        block = plane_index(i) if block is None else block
        to = device(z, (y + i // 4) % 4, (x + i % 4) % 4, k)
        return push(GB.at[block], PI.at[i], pi_s.at[i], pi_r.at[i], to)

    def pi_send(i):
        @pl.when(plane_index(i) < NB)
        def _():
            pi(i).start()

    each(1, 16, pi_send)
    sums_image = p0 < NB

    for s in range(1, 16):
        pt(s).wait_recv()
    PART[...] = dot(XTT[...], PT[...].reshape(B, Q))
    sums_text = p0 >= TEXT_AT

    def ut(u):
        at = TEXT_AT + mine
        return push(VB.at[u], UT.at[p0], ut_s.at[u], ut_r.at[p0], device(u // 2, at // 4, at % 4, u % 2))

    def ut_here(u):
        return (u // 2 == z) & (TEXT_AT + mine == p0) & (u % 2 == k)

    def ut_used(u):
        return (k == 0) | (u // 2 == z)

    def ut_send(i):
        u = (i + 2 * z + 8) % 16

        @pl.when(ut_used(u))
        def _():
            VB[u, 0:U] = PART[pl.ds(pl.multiple_of(u * U, 8), U)].astype(BF)

            @pl.when(ut_here(u))
            def _():
                UT[p0] = VB[u]

            @pl.when(jnp.logical_not(ut_here(u)))
            def _():
                ut(u).start()

    each(0, 16, ut_send)

    def cb():
        return push(SB, CB, cb_s.at[0], cb_r.at[0], sib)

    def ui(d):
        return push(UB.at[d], UI.at[d], ui_s.at[d], ui_r.at[d], device((z + d) % 8, y, x, k))

    def head_rows(zz, h):
        return pl.ds(pl.multiple_of(zz * (2 * U) + h * U, 8), U)

    @pl.when(sums_image)
    def _():
        PI[0] = GB[p0]
        each(1, 16, lambda i: pi(i, 0).wait_recv())
        PARI[...] = dot(XIT[...], PI[...].reshape(B, Q))

        def give(d):
            SB[d, 0:U] = PARI[head_rows((z + d) % 8, 1 - k)].astype(BF)

        each(0, 8, give)
        cb().start()

    out[R : 2 * R] = dot_nt(half_text, WT[...])

    @pl.when(sums_image)
    def _():
        cb().wait_recv()

        def pass_on(d):
            UB[d, 0:U] = (PARI[head_rows((z + d) % 8, k)] + CB[d, 0:U].astype(F32)).astype(BF)

            @pl.when(d > 0)
            def _():
                ui(d).start()

        each(0, 8, pass_on)

    def spread(t):
        return device(z, (y + 2 + t // 4) % 4, k * 2 + (t // 2) % 2, t % 2)

    def here(t):
        return (t // 4 == 2) & (k * 2 + (t // 2) % 2 == x) & (t % 2 == k)

    def fi(t):
        return push(CI, FI.at[p0], fi_s.at[t], fi_r.at[p0], spread(t))

    def ft(t):
        return push(CX, FT.at[p0 - TEXT_AT], ft_s.at[t], ft_r.at[p0 - TEXT_AT], spread(t))

    out[0:R] = dot_nt(half_image, WI[...])

    @pl.when(sums_image)
    def _():
        def add_image(d, acc):
            ui(d).wait_recv()
            return acc + UI[d, 0:U].astype(F32)

        CI[0:U] = lax.fori_loop(1, 8, add_image, UB[0, 0:U].astype(F32)).astype(BF)

        def send(t):
            @pl.when(here(t))
            def _():
                FI[p0] = CI[...]

            @pl.when(jnp.logical_not(here(t)))
            def _():
                fi(t).start()

        each(0, 16, send)

    @pl.when(sums_text)
    def _():
        block = p0 - TEXT_AT
        own = jnp.where(block < 8, (z == block) & (k == 0), k == 1)

        def add_text(q, acc):
            @pl.when(jnp.logical_not(own & (q == p0)))
            def _():
                push(VB.at[0], UT.at[q], ut_s.at[0], ut_r.at[q], sib).wait_recv()

            return acc + UT[q, 0:U].astype(F32)

        CX[0:U] = lax.fori_loop(0, 16, add_text, jnp.zeros((U, Q), F32)).astype(BF)

        def send(t):
            @pl.when(here(t))
            def _():
                FT[block] = CX[...]

            @pl.when(jnp.logical_not(here(t)))
            def _():
                ft(t).start()

        each(0, 16, send)

    for j in range(NB):
        lanes = slice(j * Q, (j + 1) * Q)

        @pl.when(jnp.logical_not((p0 == j) & (x // 2 == k)))
        def _():
            push(CI, FI.at[j], fi_s.at[0], fi_r.at[j], sib).wait_recv()

        out[2 * R : 2 * R + U, lanes] = FI[j, 0:U].astype(F32)

    for j in range(NB):
        lanes = slice(j * Q, (j + 1) * Q)

        @pl.when(jnp.logical_not((p0 == j + TEXT_AT) & (x // 2 == k)))
        def _():
            push(CX, FT.at[j], ft_s.at[0], ft_r.at[j], sib).wait_recv()

        out[2 * R + U :, lanes] = FT[j, 0:U].astype(F32)

    for copy in (*z_near.values(), *z_far.values(), *near_t.values(), *relay_t.values(), *half_t, *sum_t):
        copy.wait_send()
    each(0, 8, lambda s: ac(s).wait_send())
    for copy in (ax, ay, a1, a2, r1, r2, f1, f2):
        for d in (1, 2, 3):
            copy(d).wait_send()
    ct(0).wait_send()
    ct(1).wait_send()
    for s in range(1, 16):
        pt(s).wait_send()

    def pi_sent(i):
        @pl.when(plane_index(i) < NB)
        def _():
            pi(i).wait_send()

    each(1, 16, pi_sent)

    def ut_sent(u):
        @pl.when(ut_used(u) & jnp.logical_not(ut_here(u)))
        def _():
            ut(u).wait_send()

    each(0, 16, ut_sent)

    @pl.when(sums_image)
    def _():
        cb().wait_send()
        each(1, 8, lambda d: ui(d).wait_send())

        def sent(t):
            @pl.when(jnp.logical_not(here(t)))
            def _():
                fi(t).wait_send()

        each(0, 16, sent)

    @pl.when(sums_text)
    def _():
        def sent(t):
            @pl.when(jnp.logical_not(here(t)))
            def _():
                ft(t).wait_send()

        each(0, 16, sent)


def body(image_features, text_features, image_weight, text_weight, log_scale, bias):
    vmem = pl.BlockSpec(memory_space=pltpu.VMEM)
    hbm = pl.BlockSpec(memory_space=pltpu.HBM)
    v = pltpu.VMEM
    dma = pltpu.SemaphoreType.DMA
    results = pl.pallas_call(
        kernel,
        out_shape=jax.ShapeDtypeStruct((2 * R + 2 * U, W), F32),
        in_specs=[hbm, hbm, hbm, vmem, vmem],
        out_specs=vmem,
        scratch_shapes=[
            v((W, W), BF), v((W, W), BF), v((4, 4, R, W), BF), v((16, R, W), BF), v((B, W), BF), v((B, W), BF), v((B, B), BF),
            v((W, B), BF), v((W, B), BF),
            v((R, W), F32), v((R, 1), F32), v((R, W), F32), v((R, 1), F32),
            v((8, R, W), BF), v((8, R, W), BF), v((8, R, W), F32), v((5, R, W), BF),
            v((2, R, W), BF), v((2, H, W), BF), v((2, R, W), BF), v((4, R, W), BF),
            v((4, 4, R, W), BF), v((4, 4, H, W), BF), v((4, 4, H, W), BF), v((4, H, W), BF), v((4, H, W), BF), v((4, H, W), BF), v((4, H, W), BF),
            v((NB, R, Q), BF), v((16, R, Q), BF), v((NB, R, Q), BF), v((16, R, Q), BF), v((W, Q), F32), v((W, Q), F32),
            v((8, UP, Q), BF), v((8, UP, Q), BF), v((8, UP, Q), BF), v((8, UP, Q), BF), v((16, UP, Q), BF), v((16, UP, Q), BF),
            v((UP, Q), BF), v((UP, Q), BF), v((NB, UP, Q), BF), v((NB, UP, Q), BF),
            dma((4,)), dma((8,)), dma((8,)), dma((8,)), dma((8,)), *[dma((4,)) for _ in range(8)],
            dma((2,)), dma((2,)), dma((2,)), dma((2,)), dma((2,)), dma((2,)), dma((4,)), dma((4,)), *[dma((4,)) for _ in range(8)],
            dma((16,)), dma((16,)), dma((16,)), dma((16,)), dma((1,)), dma((1,)), dma((8,)), dma((8,)),
            dma((16,)), dma((16,)), dma((16,)), dma((NB,)), dma((16,)), dma((NB,)),
        ],
        compiler_params=pltpu.CompilerParams(
            collective_id=0, has_side_effects=True, vmem_limit_bytes=52 * 1024 * 1024
        ),
    )(
        jnp.stack([image_features, text_features]), image_weight, text_weight,
        log_scale.reshape(1, 1), bias.reshape(1, 1),
    )

    return results[:R], results[R : 2 * R], results[2 * R : 2 * R + U], results[2 * R + U :]


def solution(mesh):
    in_specs = (P(("row", "col"), None), P(("col", "row"), None), P(), P(), P(), P())
    out_specs = (P(("row", "col"), None), P(("col", "row"), None), P("row", None), P("row", None))
    return jax.shard_map(body, mesh=mesh, in_specs=in_specs, out_specs=out_specs, check_vma=False)
```

time: 800 us -> 73.5 us (0.09)
  waiting for transfers between devices: 745 us -> 0 us
  Pallas kernels: 0 us -> 68.8 us
  matrix products: 21.2 us -> 0 us
  between operations: 16.2 us -> 1.94 us
  local copies, waits for them, and re-layouts: 11.4 us -> 1.61 us
    reduce_scatter x2 -> x0, waiting for transfers between devices: 262 us -> none  [the longest x1 204 us: body(): lax.psum_scatter(lax.dot_general(picked, image_block, (((0,), (0,)), ((),...]
    unnamed x7 -> x0, waiting for transfers between devices: 251 us -> none
    psum x1 -> x0, waiting for transfers between devices: 119 us -> none  [body(): lax.psum(shares[0].astype(jnp.bfloat16), 'col').astype(jnp.float32)]
    all_gather x2 -> x0, waiting for transfers between devices: 114 us -> none  [the longest x1 78.8 us: body(): text_block = lax.all_gather(text_half, 'row', axis=0, tiled=True)]
    pallas_call x0 -> x1, Pallas kernels: none -> 68.8 us  [body(): pl.pallas_call(kernel, out_shape=jax.ShapeDtypeStruct((2 * R + 2 * U, W),...]
    dot_general x9 -> x0, matrix products: 21.2 us -> none  [the longest x2 5.94 us: outer_term(): lax.dot_general(features, grad_half, (((0,), (0,)), ((), ())), preferred_...]
    unnamed x23 -> x0, local copies, waits for them, and re-layouts: 11.4 us -> none
  transfers between devices with their start and end apart: 6 -> 0, of which waited for: 6 -> 0; matrix products, arithmetic and copies ran while one was open for 1% -> 0% of each run, Pallas kernels for 0% -> 0%
where the time goes in v2:
time: 73.5 us; the launch traced here: 73.3 us
  Pallas kernels  68.8 us (94%)
  between operations  1.94 us (3%)
  local copies, waits for them, and re-layouts  1.61 us (2%)
  other arithmetic  0.94 us (1%)
    pallas_call x1, Pallas kernels, body(): pl.pallas_call(kernel, out_shape=jax.ShapeDtypeStruct((2 * R + 2 * U, W),...  68.8 us

profile of v2, /device:TPU:1, one launch (start us, length us, event | category | flops | bytes accessed | tf_op | source)
XLA Modules:
  0.0 73.3 jit_solution(14487079035233885117)
XLA Ops:
  0.6 0.9 %pad_maximum_fusion.both_x = bf16[2,32,1152]{2,1,0:T(8,128)(2,1)S(1)} fusion(bf16[1,32,1152]{2,1,0:T(8,128)(2,1)} %bitcast.6, bf16[1,32,1152]{2,1,0:T(8,128)(2,1)} %bitcast.7), kind=kLoop, calls=%fused_computation | loop fusion | flops 73728 | bytes 294912 | tf_op jit(solution)/shard_map/stack | solution.py:587
  2.9 68.8 %shard_map.93 = f32[208,1152]{1,0:T(8,128)S(1)} custom-call(bf16[2,32,1152]{2,1,0:T(8,128)(2,1)S(1)} %pad_maximum_fusion.both_x, bf16[1152,1152]{1,0:T(8,128)(2,1)} %wi_hbm.1, bf16[1152,1152]{1,0:T(8,128)(2,1)} %wt_hbm.1, f32[1,1]{1,0:T(1,128)} %bitcast.4.ls, f32[1,1]{1,0:T(1,128)} %bitcast.5.bs), custom_call_target="tpu_custom_call" | custom-call | tf_op jit(solution)/shard_map/pallas_call | solution.py:563
  71.7 0.9 %fusion = (f32[72,1152]{1,0:T(8,128)}, f32[72,1152]{1,0:T(8,128)}) fusion(f32[208,1152]{1,0:T(8,128)S(1)} %shard_map.93), kind=kLoop, calls=%fused_computation.1 | loop fusion | bytes 1327104 | tf_op jit(solution)/shard_map/slice | solution.py:591
  72.6 0.7 fusion.1

commit v3 on v2

--- a/solution.py
+++ b/solution.py
@@ -16,22 +16,25 @@
 U = 72
 UP = 80
 NB = 9
-TEXT_AT = 7
-ORDER = (0, 1, 7, 2, 6, 3, 5, 4)
-POS = {d: n for n, d in enumerate(ORDER)}
+POS = {6: 0, 3: 1, 5: 2, 4: 3, 0: 8, 1: 9, 7: 10, 2: 11}
+OWN = POS[0]
+
+
+def div(a, b):
+    return a // b if isinstance(a, int) else lax.div(a, jnp.int32(b))
+
+
+def rem(a, b):
+    return a % b if isinstance(a, int) else lax.rem(a, jnp.int32(b))
 
 
 def place():
     r, c = lax.axis_index("row"), lax.axis_index("col")
-    return r // 2, c // 4, (r % 2) * 2 + (c % 4) // 2, c % 2
-
-
-def other(s):
-    return 8 + (s + 4) % 8
+    return div(r, 2), div(c, 4), rem(r, 2) * 2 + div(rem(c, 4), 2), rem(c, 2)
 
 
 def device(z, y, x, k):
-    return (z * 2 + x // 2, y * 4 + (x % 2) * 2 + k)
+    return (z * 2 + div(x, 2), y * 4 + rem(x, 2) * 2 + k)
 
 
 def push(src, dst, send, recv, to):
@@ -68,7 +71,7 @@
     ST, CT, GT, S2, RA, RB, RM, RT, SI, R1, R2, N1, N2, F1, F2,
     GB, PI, TB, PT, PARI, PART, SB, CB, UB, UI, VB, UT, CI, CX, FI, FT,
     lsem, at_s, at_r, ac_s, ac_r, ax_s, ax_r, ay_s, ay_r, a1_s, a1_r, a2_s, a2_r,
-    ct_s, ct_r, ra_s, ra_r, rb_s, rb_r, rt_s, rt_r, r1_s, r1_r, r2_s, r2_r, f1_s, f1_r, f2_s, f2_r,
+    ct_s, ct_r, ra_s, ra_r, rb_s, rb_r, rt_s, rt_r, r1_s, r1_r, r2_s, r2_r, e1_s, e1_r, e2_s, e2_r, f1_s, f1_r, f2_s, f2_r,
     pi_s, pi_r, pt_s, pt_r, cb_s, cb_r, ui_s, ui_r, ut_s, ut_r, fi_s, fi_r, ft_s, ft_r,
 ):
     z, y, x, k = place()
@@ -76,17 +79,17 @@
     sib = device(z, y, x, 1 - k)
 
     def at_z(d):
-        return device((z + d + 8) % 8, y, x, k)
+        return device(rem(z + d + 8, 8), y, x, k)
 
     def at_y(d):
-        return device(z, (y + d + 4) % 4, x, k)
+        return device(z, rem(y + d + 4, 4), x, k)
 
     def at_x(d):
-        return device(z, y, (x + d + 4) % 4, k)
+        return device(z, y, rem(x + d + 4, 4), k)
 
     loads = [
         pltpu.make_async_copy(src, dst, lsem.at[n])
-        for n, (src, dst) in enumerate(((both_x.at[1], XT.at[0]), (both_x.at[0], XI.at[0, 0]), (wt_hbm, WT), (wi_hbm, WI)))
+        for n, (src, dst) in enumerate(((both_x.at[1], XT.at[OWN]), (both_x.at[0], XI.at[0, 0]), (wt_hbm, WT), (wi_hbm, WI)))
     ]
     for load in loads:
         load.start()
@@ -116,7 +119,7 @@
     z_far = {3: tz(2, 1, 4), 5: tz(-2, -1, 5), 4: tz(2, 2, 6, 0), 12: tz(-2, -2, 7, H)}
 
     def ac(s):
-        return push(XT.at[s], XT.at[other(s)], ac_s.at[s], ac_r.at[s], sib)
+        return push(XT.at[s], XT.at[s + 4], ac_s.at[s], ac_r.at[s], sib)
 
     def ax(d):
         return push(XI.at[0, 0], XI.at[0, d], ax_s.at[d], ax_r.at[d], at_x(d))
@@ -124,13 +127,25 @@
     def ay(d):
         return push(XI.at[0, 0], XI.at[d, 0], ay_s.at[d], ay_r.at[d], at_y(d))
 
-    def a1(d):
+    def a1(d, e):
         rows = pl.ds(0, H)
-        return push(XI.at[0, 1:4, rows], XI.at[d, 1:4, rows], a1_s.at[d], a1_r.at[d], at_y(d))
-
-    def a2(d):
+        n = 4 * d + e
+        return push(XI.at[0, e, rows], XI.at[d, e, rows], a1_s.at[n], a1_r.at[n], at_y(d))
+
+    def a2(d, e):
         rows = pl.ds(H, H)
-        return push(XI.at[1:4, 0, rows], XI.at[1:4, d, rows], a2_s.at[d], a2_r.at[d], at_x(d))
+        n = 4 * d + e
+        return push(XI.at[e, 0, rows], XI.at[e, d, rows], a2_s.at[n], a2_r.at[n], at_x(d))
+
+    def relay_x(e):
+        ax(e).wait_recv()
+        for d in (2, 1, 3):
+            a1(d, e).start()
+
+    def relay_y(e):
+        ay(e).wait_recv()
+        for d in (2, 1, 3):
+            a2(d, e).start()
 
     z_near[2].start()
     z_near[6].start()
@@ -139,7 +154,7 @@
         ay(d).start()
     z_near[1].start()
     z_near[7].start()
-    ac(0).start()
+    ac(OWN).start()
 
     def project(x_in, n, WW, HH, c):
         p = dot(x_in.reshape(n * Q, W), WW[...])
@@ -152,29 +167,25 @@
         for copy in copies:
             copy.wait_recv()
 
-    def relay():
-        z_near[2].wait_recv()
-        z_far[4].start()
-        z_far[3].start()
-        ac(POS[2]).start()
-        z_near[6].wait_recv()
-        z_far[12].start()
-        z_far[5].start()
-        ac(POS[6]).start()
-        for d in (1, 7):
-            z_near[d].wait_recv()
-            ac(POS[d]).start()
-
-    relay()
-    arrived(ax(d) for d in (1, 3, 2))
-    for d in (2, 1, 3):
-        a1(d).start()
-    arrived(ay(d) for d in (1, 3, 2))
-    for d in (2, 1, 3):
-        a2(d).start()
+    for e in (1, 3):
+        relay_x(e)
+        relay_y(e)
+    z_near[2].wait_recv()
+    z_far[4].start()
+    z_far[3].start()
+    ac(POS[2]).start()
+    z_near[6].wait_recv()
+    z_far[12].start()
+    z_far[5].start()
+    relay_x(2)
+    relay_y(2)
+    ac(POS[6]).start()
+    for d in (1, 7):
+        z_near[d].wait_recv()
+        ac(POS[d]).start()
 
     loads[2].wait()
-    p, length = project(XT[0:4], 1, WT, HT, 0)
+    p, length = project(XT[8:12], 1, WT, HT, 2)
     DT[...] = p[:R]
     LT[...] = length[:R]
     loads[3].wait()
@@ -188,24 +199,23 @@
     ac(POS[5]).start()
     arrived([z_far[4], z_far[12]])
     ac(POS[4]).start()
+    arrived(ac(s) for s in (8, 9, 10, 11))
+    project(XT[12:16], 1, WT, HT, 3)
     arrived(ac(s) for s in range(4))
-    project(XT[12:16], 1, WT, HT, 3)
-    arrived(a2(d) for d in (1, 2, 3))
-    arrived(a1(d) for d in (1, 3, 2))
+    project(XT[0:8], 2, WT, HT, 0)
+    arrived(a(d, e) for a in (a1, a2) for d in (1, 3, 2) for e in (1, 3, 2))
     project(XI[1:4], 3, WI, HI, 1)
-    arrived(ac(s) for s in range(4, 8))
-    project(XT[4:12], 2, WT, HT, 1)
 
     factor = jnp.exp(ls[...])
     bias = bs[...]
     col = lax.broadcasted_iota(jnp.int32, (1, B), 1)
     cs = col >> 5
     cd = jnp.zeros_like(cs)
-    for n, d in enumerate(ORDER):
-        cd = jnp.where((cs == n) | (cs == other(n)), d, cd)
+    for d, n in POS.items():
+        cd = jnp.where((cs & 11) == n, d, cd)
     cz = (z - cd) & 7
-    ck = k ^ (cs >> 3)
-    tid = (y * 4 + (x % 2) * 2 + ck) * B + (cz * 2 + x // 2) * R + (col & 31)
+    ck = k ^ ((cs >> 2) & 1)
+    tid = (y * 4 + rem(x, 2) * 2 + ck) * B + (cz * 2 + div(x, 2)) * R + (col & 31)
     row = lax.broadcasted_iota(jnp.int32, (B, 1), 0)
     rs = row >> 5
     ry = (y - (rs >> 2)) & 3
@@ -235,15 +245,15 @@
     sum_t = [push(RM.at[n], RT.at[2 + n], rt_s.at[2 + n], rt_r.at[2 + n], at_z(2 * (2 * n - 1))) for n in (0, 1)]
 
     def both(d):
-        return GT[POS[d]] + CT[POS[d]].astype(F32)
-
-    pair(1, 2)
-    ST[4:8] = text_grad(2).astype(BF)
-    ct(1).start()
-    GT[4:8] = text_grad(1)
-    pair(0, 1)
-    pair(3, 1)
-    ct(1).wait_recv()
+        n = POS[d] if POS[d] < 4 else POS[d] - 4
+        return GT[n] + CT[n].astype(F32)
+
+    pair(0, 2)
+    ST[0:4] = text_grad(1).astype(BF)
+    ct(0).start()
+    GT[0:4] = text_grad(0)
+    pair(2, 2)
+    ct(0).wait_recv()
     S2[4] = both(4).astype(BF)
     half_t[0].start()
     half_t[1].start()
@@ -251,24 +261,31 @@
     relay_t[3].start()
     S2[3] = both(5).astype(BF)
     relay_t[5].start()
-    ST[0:4] = text_grad(3).astype(BF)
-    ct(0).start()
+    ST[4:8] = text_grad(3).astype(BF)
+    ct(1).start()
 
     def r1(d):
-        return push(SI.at[d, :, pl.ds(0, H)], R1.at[d], r1_s.at[d], r1_r.at[d], at_y(-d))
+        return push(SI.at[d, 1:4, pl.ds(0, H)], R1.at[d, 1:4], r1_s.at[d], r1_r.at[d], at_y(-d))
 
     def r2(d):
-        return push(SI.at[:, d, pl.ds(H, H)], R2.at[d], r2_s.at[d], r2_r.at[d], at_x(-d))
-
-    for c in (2, 1, 3, 0):
-        SI[c] = dot(PW[c * Q : (c + 1) * Q], HT[...]).astype(BF).reshape(4, R, W)
-        if c > 0:
-            r1(c).start()
+        return push(SI.at[1:4, d, pl.ds(H, H)], R2.at[d, 1:4], r2_s.at[d], r2_r.at[d], at_x(-d))
+
+    def e1(d):
+        return push(SI.at[d, 0, pl.ds(0, H)], R1.at[d, 0], e1_s.at[d], e1_r.at[d], at_y(-d))
+
+    def e2(d):
+        return push(SI.at[0, d, pl.ds(H, H)], R2.at[d, 0], e2_s.at[d], e2_r.at[d], at_x(-d))
+
+    SI[...] = dot(PW[...], HT[...]).astype(BF).reshape(4, 4, R, W)
     for d in (2, 1, 3):
+        r1(d).start()
         r2(d).start()
-
-    GT[0:4] = text_grad(0)
-    ct(0).wait_recv()
+    for d in (2, 1, 3):
+        e1(d).start()
+        e2(d).start()
+
+    GT[4:8] = text_grad(2)
+    ct(1).wait_recv()
     S2[0] = both(1).astype(BF)
     near_t[1].start()
     S2[1] = both(7).astype(BF)
@@ -308,12 +325,10 @@
     for d in (2, 1, 3):
         sum1(d)
         f1(d).start()
-    sum1(0)
     arrived(r2(d) for d in (1, 3, 2))
     for d in (2, 1, 3):
         sum2(d)
         f2(d).start()
-    sum2(0)
 
     def unembed(g, D, L, blocks):
         d = D[...]
@@ -330,15 +345,19 @@
     mine = jnp.where(k == 0, z, 8)
 
     def pt(s):
-        zz = (z + s % 8) % 8
-        kk = (k + s // 8) % 2
-        slot = POS[s % 8] if s < 8 else other(POS[s % 8])
+        zz = rem(z + s % 8, 8)
+        kk = rem(k + s // 8, 2)
+        slot = POS[s % 8] + 4 * (s // 8)
         return push(TB.at[jnp.where(kk == 0, zz, 8)], PT.at[slot], pt_s.at[s], pt_r.at[s], device(zz, y, x, kk))
 
     for s in range(1, 16):
         pt(s).start()
-    PT[0] = TB[mine]
-
+    PT[OWN] = TB[mine]
+
+    arrived(e1(d) for d in (1, 3, 2))
+    sum1(0)
+    arrived(e2(d) for d in (1, 3, 2))
+    sum2(0)
     arrived(f1(d) for d in (1, 3, 2))
     arrived(f2(d) for d in (1, 3, 2))
     g1 = N1[0].astype(F32)
@@ -349,11 +368,11 @@
     half_image = unembed(jnp.concatenate([g1, g2], axis=0), DI, LI, GB)
 
     def plane_index(i):
-        return ((y + i // 4) % 4) * 4 + (x + i % 4) % 4
+        return rem(y + div(i, 4), 4) * 4 + rem(x + rem(i, 4), 4)
 
     def pi(i, block=None):
         block = plane_index(i) if block is None else block
-        to = device(z, (y + i // 4) % 4, (x + i % 4) % 4, k)
+        to = device(z, rem(y + div(i, 4), 4), rem(x + rem(i, 4), 4), k)
         return push(GB.at[block], PI.at[i], pi_s.at[i], pi_r.at[i], to)
 
     def pi_send(i):
@@ -367,20 +386,26 @@
     for s in range(1, 16):
         pt(s).wait_recv()
     PART[...] = dot(XTT[...], PT[...].reshape(B, Q))
-    sums_text = p0 >= TEXT_AT
+    m, h = 2 * y + rem(x, 2), div(x, 2)
+    zt = rem(m + 8 - z, 8)
+    sums_text = (k == 0) | (m == z)
+
+    def ut_place(u):
+        return jnp.where(k == 0, rem(div(u, 2) + z, 8), z)
 
     def ut(u):
-        at = TEXT_AT + mine
-        return push(VB.at[u], UT.at[p0], ut_s.at[u], ut_r.at[p0], device(u // 2, at // 4, at % 4, u % 2))
+        at = ut_place(u)
+        to = device(z, div(at, 2), 2 * rem(u, 2) + rem(at, 2), k)
+        return push(VB.at[u], UT.at[p0], ut_s.at[u], ut_r.at[p0], to)
 
     def ut_here(u):
-        return (u // 2 == z) & (TEXT_AT + mine == p0) & (u % 2 == k)
+        return (ut_place(u) == m) & (rem(u, 2) == h)
 
     def ut_used(u):
-        return (k == 0) | (u // 2 == z)
+        return (k == 0) | (div(u, 2) == z)
 
     def ut_send(i):
-        u = (i + 2 * z + 8) % 16
+        u = rem(i + 2 * zt + 8, 16)
 
         @pl.when(ut_used(u))
         def _():
@@ -400,7 +425,7 @@
         return push(SB, CB, cb_s.at[0], cb_r.at[0], sib)
 
     def ui(d):
-        return push(UB.at[d], UI.at[d], ui_s.at[d], ui_r.at[d], device((z + d) % 8, y, x, k))
+        return push(UB.at[d], UI.at[d], ui_s.at[d], ui_r.at[d], device(rem(z + d, 8), y, x, k))
 
     def head_rows(zz, h):
         return pl.ds(pl.multiple_of(zz * (2 * U) + h * U, 8), U)
@@ -412,7 +437,7 @@
         PARI[...] = dot(XIT[...], PI[...].reshape(B, Q))
 
         def give(d):
-            SB[d, 0:U] = PARI[head_rows((z + d) % 8, 1 - k)].astype(BF)
+            SB[d, 0:U] = PARI[head_rows(rem(z + d, 8), 1 - k)].astype(BF)
 
         each(0, 8, give)
         cb().start()
@@ -423,95 +448,25 @@
     def _():
         cb().wait_recv()
 
-        def pass_on(d):
-            UB[d, 0:U] = (PARI[head_rows((z + d) % 8, k)] + CB[d, 0:U].astype(F32)).astype(BF)
+        def pass_on(i):
+            d = rem(i + 4, 8)
+            UB[d, 0:U] = (PARI[head_rows(rem(z + d, 8), k)] + CB[d, 0:U].astype(F32)).astype(BF)
 
             @pl.when(d > 0)
             def _():
                 ui(d).start()
 
         each(0, 8, pass_on)
-
-    def spread(t):
-        return device(z, (y + 2 + t // 4) % 4, k * 2 + (t // 2) % 2, t % 2)
-
-    def here(t):
-        return (t // 4 == 2) & (k * 2 + (t // 2) % 2 == x) & (t % 2 == k)
-
-    def fi(t):
-        return push(CI, FI.at[p0], fi_s.at[t], fi_r.at[p0], spread(t))
-
-    def ft(t):
-        return push(CX, FT.at[p0 - TEXT_AT], ft_s.at[t], ft_r.at[p0 - TEXT_AT], spread(t))
-
-    out[0:R] = dot_nt(half_image, WI[...])
-
-    @pl.when(sums_image)
-    def _():
-        def add_image(d, acc):
-            ui(d).wait_recv()
-            return acc + UI[d, 0:U].astype(F32)
-
-        CI[0:U] = lax.fori_loop(1, 8, add_image, UB[0, 0:U].astype(F32)).astype(BF)
-
-        def send(t):
-            @pl.when(here(t))
-            def _():
-                FI[p0] = CI[...]
-
-            @pl.when(jnp.logical_not(here(t)))
-            def _():
-                fi(t).start()
-
-        each(0, 16, send)
-
-    @pl.when(sums_text)
-    def _():
-        block = p0 - TEXT_AT
-        own = jnp.where(block < 8, (z == block) & (k == 0), k == 1)
-
-        def add_text(q, acc):
-            @pl.when(jnp.logical_not(own & (q == p0)))
-            def _():
-                push(VB.at[0], UT.at[q], ut_s.at[0], ut_r.at[q], sib).wait_recv()
-
-            return acc + UT[q, 0:U].astype(F32)
-
-        CX[0:U] = lax.fori_loop(0, 16, add_text, jnp.zeros((U, Q), F32)).astype(BF)
-
-        def send(t):
-            @pl.when(here(t))
-            def _():
-                FT[block] = CX[...]
-
-            @pl.when(jnp.logical_not(here(t)))
-            def _():
-                ft(t).start()
-
-        each(0, 16, send)
-
-    for j in range(NB):
-        lanes = slice(j * Q, (j + 1) * Q)
-
-        @pl.when(jnp.logical_not((p0 == j) & (x // 2 == k)))
-        def _():
-            push(CI, FI.at[j], fi_s.at[0], fi_r.at[j], sib).wait_recv()
-
-        out[2 * R : 2 * R + U, lanes] = FI[j, 0:U].astype(F32)
-
-    for j in range(NB):
-        lanes = slice(j * Q, (j + 1) * Q)
-
-        @pl.when(jnp.logical_not((p0 == j + TEXT_AT) & (x // 2 == k)))
-        def _():
-            push(CX, FT.at[j], ft_s.at[0], ft_r.at[j], sib).wait_recv()
-
-        out[2 * R + U :, lanes] = FT[j, 0:U].astype(F32)
 
     for copy in (*z_near.values(), *z_far.values(), *near_t.values(), *relay_t.values(), *half_t, *sum_t):
         copy.wait_send()
-    each(0, 8, lambda s: ac(s).wait_send())
-    for copy in (ax, ay, a1, a2, r1, r2, f1, f2):
+    for n in POS.values():
+        ac(n).wait_send()
+    for copy in (a1, a2):
+        for d in (1, 2, 3):
+            for e in (1, 2, 3):
+                copy(d, e).wait_send()
+    for copy in (ax, ay, r1, r2, e1, e2, f1, f2):
         for d in (1, 2, 3):
             copy(d).wait_send()
     ct(0).wait_send()
@@ -522,14 +477,94 @@
     def pi_sent(i):
         @pl.when(plane_index(i) < NB)
         def _():
-            pi(i).wait_send()
+            pi(i, 0).wait_send()
 
     each(1, 16, pi_sent)
+
+    block = jnp.where(k == 0, z, 8)
+    zd = jnp.where(k == 0, zt, z)
+
+    def ft(t):
+        to = device(zd, rem(y + 2 + div(t, 4), 4), 2 * h + rem(div(t, 2), 2), rem(t, 2))
+        return push(CX, FT.at[block], ft_s.at[t], ft_r.at[block], to)
+
+    def ft_here(t):
+        return (zd == z) & (div(t, 4) == 2) & (rem(div(t, 2), 2) == rem(x, 2)) & (rem(t, 2) == k)
+
+    def fi(t):
+        to = device(z, rem(y + 2 + div(t, 4), 4), k * 2 + rem(div(t, 2), 2), rem(t, 2))
+        return push(CI, FI.at[p0], fi_s.at[t], fi_r.at[p0], to)
+
+    def fi_here(t):
+        return (div(t, 4) == 2) & (k * 2 + rem(div(t, 2), 2) == x) & (rem(t, 2) == k)
+
+    @pl.when(sums_text)
+    def _():
+        def add_text(q, acc):
+            @pl.when(q != p0)
+            def _():
+                push(VB.at[0], UT.at[q], ut_s.at[0], ut_r.at[q], sib).wait_recv()
+
+            return acc + UT[q, 0:U].astype(F32)
+
+        CX[0:U] = lax.fori_loop(0, 16, add_text, jnp.zeros((U, Q), F32)).astype(BF)
+
+        def send(t):
+            @pl.when(ft_here(t))
+            def _():
+                FT[block] = CX[...]
+
+            @pl.when(jnp.logical_not(ft_here(t)))
+            def _():
+                ft(t).start()
+
+        each(0, 16, send)
+
+    out[0:R] = dot_nt(half_image, WI[...])
+
+    @pl.when(sums_image)
+    def _():
+        def add_image(d, acc):
+            ui(d).wait_recv()
+            return acc + UI[d, 0:U].astype(F32)
+
+        CI[0:U] = lax.fori_loop(1, 8, add_image, UB[0, 0:U].astype(F32)).astype(BF)
+
+        def send(t):
+            @pl.when(fi_here(t))
+            def _():
+                FI[p0] = CI[...]
+
+            @pl.when(jnp.logical_not(fi_here(t)))
+            def _():
+                fi(t).start()
+
+        each(0, 16, send)
+
+    for j in range(NB):
+        lanes = slice(j * Q, (j + 1) * Q)
+
+        mine_j = ((k == 1) & (m == z)) if j == 8 else ((k == 0) & (z == j) & (zt == z))
+
+        @pl.when(jnp.logical_not(mine_j))
+        def _():
+            push(CX, FT.at[j], ft_s.at[0], ft_r.at[j], sib).wait_recv()
+
+        out[2 * R + U :, lanes] = FT[j, 0:U].astype(F32)
+
+    for j in range(NB):
+        lanes = slice(j * Q, (j + 1) * Q)
+
+        @pl.when(jnp.logical_not((p0 == j) & (h == k)))
+        def _():
+            push(CI, FI.at[j], fi_s.at[0], fi_r.at[j], sib).wait_recv()
+
+        out[2 * R : 2 * R + U, lanes] = FI[j, 0:U].astype(F32)
 
     def ut_sent(u):
         @pl.when(ut_used(u) & jnp.logical_not(ut_here(u)))
         def _():
-            ut(u).wait_send()
+            push(VB.at[0], UT.at[0], ut_s.at[u], ut_r.at[0], sib).wait_send()
 
     each(0, 16, ut_sent)
 
@@ -539,18 +574,18 @@
         each(1, 8, lambda d: ui(d).wait_send())
 
         def sent(t):
-            @pl.when(jnp.logical_not(here(t)))
-            def _():
-                fi(t).wait_send()
+            @pl.when(jnp.logical_not(fi_here(t)))
+            def _():
+                push(CI, FI.at[0], fi_s.at[t], fi_r.at[0], sib).wait_send()
 
         each(0, 16, sent)
 
     @pl.when(sums_text)
     def _():
         def sent(t):
-            @pl.when(jnp.logical_not(here(t)))
-            def _():
-                ft(t).wait_send()
+            @pl.when(jnp.logical_not(ft_here(t)))
+            def _():
+                push(CX, FT.at[0], ft_s.at[t], ft_r.at[0], sib).wait_send()
 
         each(0, 16, sent)
 
@@ -575,8 +610,8 @@
             v((NB, R, Q), BF), v((16, R, Q), BF), v((NB, R, Q), BF), v((16, R, Q), BF), v((W, Q), F32), v((W, Q), F32),
             v((8, UP, Q), BF), v((8, UP, Q), BF), v((8, UP, Q), BF), v((8, UP, Q), BF), v((16, UP, Q), BF), v((16, UP, Q), BF),
             v((UP, Q), BF), v((UP, Q), BF), v((NB, UP, Q), BF), v((NB, UP, Q), BF),
-            dma((4,)), dma((8,)), dma((8,)), dma((8,)), dma((8,)), *[dma((4,)) for _ in range(8)],
-            dma((2,)), dma((2,)), dma((2,)), dma((2,)), dma((2,)), dma((2,)), dma((4,)), dma((4,)), *[dma((4,)) for _ in range(8)],
+            dma((4,)), dma((8,)), dma((8,)), dma((12,)), dma((12,)), *[dma((4,)) for _ in range(4)], *[dma((16,)) for _ in range(4)],
+            dma((2,)), dma((2,)), dma((2,)), dma((2,)), dma((2,)), dma((2,)), dma((4,)), dma((4,)), *[dma((4,)) for _ in range(12)],
             dma((16,)), dma((16,)), dma((16,)), dma((16,)), dma((1,)), dma((1,)), dma((8,)), dma((8,)),
             dma((16,)), dma((16,)), dma((16,)), dma((NB,)), dma((16,)), dma((NB,)),
         ],

time: 73.5 us -> 69.2 us (0.941)
  Pallas kernels: 68.8 us -> 64.6 us
    pallas_call x1, Pallas kernels: 68.8 us -> 64.6 us  [body(): pl.pallas_call(kernel, out_shape=jax.ShapeDtypeStruct((2 * R + 2 * U, W),...]
where the time goes in v3:
time: 69.2 us; the launch traced here: 69.1 us
  Pallas kernels  64.6 us (93%)
  between operations  1.94 us (3%)
  local copies, waits for them, and re-layouts  1.61 us (2%)
  other arithmetic  0.94 us (1%)
    pallas_call x1, Pallas kernels, body(): pl.pallas_call(kernel, out_shape=jax.ShapeDtypeStruct((2 * R + 2 * U, W),...  64.6 us

profile of v3, /device:TPU:1, one launch (start us, length us, event | category | flops | bytes accessed | tf_op | source)
XLA Modules:
  0.0 69.1 jit_solution(5261496411763881479)
XLA Ops:
  0.6 0.9 %pad_maximum_fusion.both_x = bf16[2,32,1152]{2,1,0:T(8,128)(2,1)S(1)} fusion(bf16[1,32,1152]{2,1,0:T(8,128)(2,1)} %bitcast.6, bf16[1,32,1152]{2,1,0:T(8,128)(2,1)} %bitcast.7), kind=kLoop, calls=%fused_computation | loop fusion | flops 73728 | bytes 294912 | tf_op jit(solution)/shard_map/stack | solution.py:622
  2.9 64.6 %shard_map.93 = f32[208,1152]{1,0:T(8,128)S(1)} custom-call(bf16[2,32,1152]{2,1,0:T(8,128)(2,1)S(1)} %pad_maximum_fusion.both_x, bf16[1152,1152]{1,0:T(8,128)(2,1)} %wi_hbm.1, bf16[1152,1152]{1,0:T(8,128)(2,1)} %wt_hbm.1, f32[1,1]{1,0:T(1,128)} %bitcast.4.ls, f32[1,1]{1,0:T(1,128)} %bitcast.5.bs), custom_call_target="tpu_custom_call" | custom-call | tf_op jit(solution)/shard_map/pallas_call | solution.py:598
  67.5 0.9 %fusion = (f32[72,1152]{1,0:T(8,128)}, f32[72,1152]{1,0:T(8,128)}) fusion(f32[208,1152]{1,0:T(8,128)S(1)} %shard_map.93), kind=kLoop, calls=%fused_computation.1 | loop fusion | bytes 1327104 | tf_op jit(solution)/shard_map/slice | solution.py:626
  68.4 0.7 %fusion.1 = (f32[32,1152]{1,0:T(8,128)}, f32[32,1152]{1,0:T(8,128)}) fusion(f32[208,1152]{1,0:T(8,128)S(1)} %shard_map.93), kind=kLoop, calls=%fused_computation.2 | loop fusion | bytes 589824 | tf_op jit(solution)/shard_map/slice | solution.py:626

commit v4 on v3

--- a/solution.py
+++ b/solution.py
@@ -64,7 +64,7 @@
 
 
 def kernel(
-    both_x, wi_hbm, wt_hbm, ls, bs,
+    xi, xt, wi_hbm, wt_hbm, ls, bs,
     out,
     WI, WT, XI, XT, HI, HT, PW, XIT, XTT,
     DI, LI, DT, LT,
@@ -89,7 +89,7 @@
 
     loads = [
         pltpu.make_async_copy(src, dst, lsem.at[n])
-        for n, (src, dst) in enumerate(((both_x.at[1], XT.at[OWN]), (both_x.at[0], XI.at[0, 0]), (wt_hbm, WT), (wi_hbm, WI)))
+        for n, (src, dst) in enumerate(((xt, XT.at[OWN]), (xi, XI.at[0, 0]), (wt_hbm, WT), (wi_hbm, WI)))
     ]
     for load in loads:
         load.start()
@@ -127,25 +127,13 @@
     def ay(d):
         return push(XI.at[0, 0], XI.at[d, 0], ay_s.at[d], ay_r.at[d], at_y(d))
 
-    def a1(d, e):
+    def a1(d):
         rows = pl.ds(0, H)
-        n = 4 * d + e
-        return push(XI.at[0, e, rows], XI.at[d, e, rows], a1_s.at[n], a1_r.at[n], at_y(d))
-
-    def a2(d, e):
+        return push(XI.at[0, 1:4, rows], XI.at[d, 1:4, rows], a1_s.at[d], a1_r.at[d], at_y(d))
+
+    def a2(d):
         rows = pl.ds(H, H)
-        n = 4 * d + e
-        return push(XI.at[e, 0, rows], XI.at[e, d, rows], a2_s.at[n], a2_r.at[n], at_x(d))
-
-    def relay_x(e):
-        ax(e).wait_recv()
-        for d in (2, 1, 3):
-            a1(d, e).start()
-
-    def relay_y(e):
-        ay(e).wait_recv()
-        for d in (2, 1, 3):
-            a2(d, e).start()
+        return push(XI.at[1:4, 0, rows], XI.at[1:4, d, rows], a2_s.at[d], a2_r.at[d], at_x(d))
 
     z_near[2].start()
     z_near[6].start()
@@ -167,9 +155,6 @@
         for copy in copies:
             copy.wait_recv()
 
-    for e in (1, 3):
-        relay_x(e)
-        relay_y(e)
     z_near[2].wait_recv()
     z_far[4].start()
     z_far[3].start()
@@ -177,8 +162,12 @@
     z_near[6].wait_recv()
     z_far[12].start()
     z_far[5].start()
-    relay_x(2)
-    relay_y(2)
+    arrived(ax(d) for d in (1, 3, 2))
+    for d in (2, 1, 3):
+        a1(d).start()
+    arrived(ay(d) for d in (1, 3, 2))
+    for d in (2, 1, 3):
+        a2(d).start()
     ac(POS[6]).start()
     for d in (1, 7):
         z_near[d].wait_recv()
@@ -203,7 +192,7 @@
     project(XT[12:16], 1, WT, HT, 3)
     arrived(ac(s) for s in range(4))
     project(XT[0:8], 2, WT, HT, 0)
-    arrived(a(d, e) for a in (a1, a2) for d in (1, 3, 2) for e in (1, 3, 2))
+    arrived(a(d) for a in (a1, a2) for d in (1, 3, 2))
     project(XI[1:4], 3, WI, HI, 1)
 
     factor = jnp.exp(ls[...])
@@ -350,7 +339,7 @@
         slot = POS[s % 8] + 4 * (s // 8)
         return push(TB.at[jnp.where(kk == 0, zz, 8)], PT.at[slot], pt_s.at[s], pt_r.at[s], device(zz, y, x, kk))
 
-    for s in range(1, 16):
+    for s in (12, 11, 13, 4, 3, 5, 10, 14, 2, 6, 9, 15, 1, 7, 8):
         pt(s).start()
     PT[OWN] = TB[mine]
 
@@ -405,7 +394,7 @@
         return (k == 0) | (div(u, 2) == z)
 
     def ut_send(i):
-        u = rem(i + 2 * zt + 8, 16)
+        u = rem(i + 2 * zt + 6, 16)
 
         @pl.when(ut_used(u))
         def _():
@@ -462,11 +451,7 @@
         copy.wait_send()
     for n in POS.values():
         ac(n).wait_send()
-    for copy in (a1, a2):
-        for d in (1, 2, 3):
-            for e in (1, 2, 3):
-                copy(d, e).wait_send()
-    for copy in (ax, ay, r1, r2, e1, e2, f1, f2):
+    for copy in (ax, ay, a1, a2, r1, r2, e1, e2, f1, f2):
         for d in (1, 2, 3):
             copy(d).wait_send()
     ct(0).wait_send()
@@ -552,15 +537,6 @@
 
         out[2 * R + U :, lanes] = FT[j, 0:U].astype(F32)
 
-    for j in range(NB):
-        lanes = slice(j * Q, (j + 1) * Q)
-
-        @pl.when(jnp.logical_not((p0 == j) & (h == k)))
-        def _():
-            push(CI, FI.at[j], fi_s.at[0], fi_r.at[j], sib).wait_recv()
-
-        out[2 * R : 2 * R + U, lanes] = FI[j, 0:U].astype(F32)
-
     def ut_sent(u):
         @pl.when(ut_used(u) & jnp.logical_not(ut_here(u)))
         def _():
@@ -573,19 +549,30 @@
         cb().wait_send()
         each(1, 8, lambda d: ui(d).wait_send())
 
-        def sent(t):
-            @pl.when(jnp.logical_not(fi_here(t)))
-            def _():
-                push(CI, FI.at[0], fi_s.at[t], fi_r.at[0], sib).wait_send()
-
-        each(0, 16, sent)
-
     @pl.when(sums_text)
     def _():
         def sent(t):
             @pl.when(jnp.logical_not(ft_here(t)))
             def _():
                 push(CX, FT.at[0], ft_s.at[t], ft_r.at[0], sib).wait_send()
+
+        each(0, 16, sent)
+
+    for j in range(NB):
+        lanes = slice(j * Q, (j + 1) * Q)
+
+        @pl.when(jnp.logical_not((p0 == j) & (h == k)))
+        def _():
+            push(CI, FI.at[j], fi_s.at[0], fi_r.at[j], sib).wait_recv()
+
+        out[2 * R : 2 * R + U, lanes] = FI[j, 0:U].astype(F32)
+
+    @pl.when(sums_image)
+    def _():
+        def sent(t):
+            @pl.when(jnp.logical_not(fi_here(t)))
+            def _():
+                push(CI, FI.at[0], fi_s.at[t], fi_r.at[0], sib).wait_send()
 
         each(0, 16, sent)
 
@@ -598,7 +585,7 @@
     results = pl.pallas_call(
         kernel,
         out_shape=jax.ShapeDtypeStruct((2 * R + 2 * U, W), F32),
-        in_specs=[hbm, hbm, hbm, vmem, vmem],
+        in_specs=[hbm, hbm, hbm, hbm, vmem, vmem],
         out_specs=vmem,
         scratch_shapes=[
             v((W, W), BF), v((W, W), BF), v((4, 4, R, W), BF), v((16, R, W), BF), v((B, W), BF), v((B, W), BF), v((B, B), BF),
@@ -610,7 +597,7 @@
             v((NB, R, Q), BF), v((16, R, Q), BF), v((NB, R, Q), BF), v((16, R, Q), BF), v((W, Q), F32), v((W, Q), F32),
             v((8, UP, Q), BF), v((8, UP, Q), BF), v((8, UP, Q), BF), v((8, UP, Q), BF), v((16, UP, Q), BF), v((16, UP, Q), BF),
             v((UP, Q), BF), v((UP, Q), BF), v((NB, UP, Q), BF), v((NB, UP, Q), BF),
-            dma((4,)), dma((8,)), dma((8,)), dma((12,)), dma((12,)), *[dma((4,)) for _ in range(4)], *[dma((16,)) for _ in range(4)],
+            dma((4,)), dma((8,)), dma((8,)), dma((12,)), dma((12,)), *[dma((4,)) for _ in range(8)],
             dma((2,)), dma((2,)), dma((2,)), dma((2,)), dma((2,)), dma((2,)), dma((4,)), dma((4,)), *[dma((4,)) for _ in range(12)],
             dma((16,)), dma((16,)), dma((16,)), dma((16,)), dma((1,)), dma((1,)), dma((8,)), dma((8,)),
             dma((16,)), dma((16,)), dma((16,)), dma((NB,)), dma((16,)), dma((NB,)),
@@ -619,7 +606,7 @@
             collective_id=0, has_side_effects=True, vmem_limit_bytes=52 * 1024 * 1024
         ),
     )(
-        jnp.stack([image_features, text_features]), image_weight, text_weight,
+        pltpu.with_memory_space_constraint(image_features, pltpu.HBM), pltpu.with_memory_space_constraint(text_features, pltpu.HBM), image_weight, text_weight,
         log_scale.reshape(1, 1), bias.reshape(1, 1),
     )
 

time: 69.2 us -> 67.4 us (0.974)
  other arithmetic: 0.94 us -> 0 us
  Pallas kernels: 64.6 us -> 63.7 us
    another operation x1 -> x0, other arithmetic: 0.94 us -> none  [body(): jnp.stack([image_features, text_features])]
    pallas_call x1, Pallas kernels: 64.6 us -> 63.7 us  [body(): pl.pallas_call(kernel, out_shape=jax.ShapeDtypeStruct((2 * R + 2 * U, W),...]
where the time goes in v4:
time: 67.4 us; the launch traced here: 67.3 us
  Pallas kernels  63.7 us (95%)
  between operations  1.93 us (3%)
  local copies, waits for them, and re-layouts  1.61 us (2%)
    pallas_call x1, Pallas kernels, body(): pl.pallas_call(kernel, out_shape=jax.ShapeDtypeStruct((2 * R + 2 * U, W),...  63.7 us

profile of v4, /device:TPU:1, one launch (start us, length us, event | category | flops | bytes accessed | tf_op | source)
XLA Modules:
  0.0 67.3 jit_solution(17059522762471699124)
XLA Ops:
  1.9 63.7 %shard_map.93 = f32[208,1152]{1,0:T(8,128)S(1)} custom-call(bf16[32,1152]{1,0:T(8,128)(2,1)} %xi.1, bf16[32,1152]{1,0:T(8,128)(2,1)} %xt.1, bf16[1152,1152]{1,0:T(8,128)(2,1)} %wi_hbm.1, bf16[1152,1152]{1,0:T(8,128)(2,1)} %wt_hbm.1, f32[1,1]{1,0:T(1,128)} %bitcast.2.ls, f32[1,1]{1,0:T(1,128)} %bitcast.3.bs), custom_call_target="tpu_custom_call" | custom-call | tf_op jit(solution)/shard_map/pallas_call | solution.py:585
  65.6 0.9 %fusion = (f32[72,1152]{1,0:T(8,128)}, f32[72,1152]{1,0:T(8,128)}) fusion(f32[208,1152]{1,0:T(8,128)S(1)} %shard_map.93), kind=kLoop, calls=%fused_computation | loop fusion | bytes 1327104 | tf_op jit(solution)/shard_map/slice | solution.py:613
  66.5 0.7 %fusion.1 = (f32[32,1152]{1,0:T(8,128)}, f32[32,1152]{1,0:T(8,128)}) fusion(f32[208,1152]{1,0:T(8,128)S(1)} %shard_map.93), kind=kLoop, calls=%fused_computation.1 | loop fusion | bytes 589824 | tf_op jit(solution)/shard_map/slice | solution.py:613

commit v5 on v4

--- a/solution.py
+++ b/solution.py
@@ -72,7 +72,7 @@
     GB, PI, TB, PT, PARI, PART, SB, CB, UB, UI, VB, UT, CI, CX, FI, FT,
     lsem, at_s, at_r, ac_s, ac_r, ax_s, ax_r, ay_s, ay_r, a1_s, a1_r, a2_s, a2_r,
     ct_s, ct_r, ra_s, ra_r, rb_s, rb_r, rt_s, rt_r, r1_s, r1_r, r2_s, r2_r, e1_s, e1_r, e2_s, e2_r, f1_s, f1_r, f2_s, f2_r,
-    pi_s, pi_r, pt_s, pt_r, cb_s, cb_r, ui_s, ui_r, ut_s, ut_r, fi_s, fi_r, ft_s, ft_r,
+    pi_s, pi_r, pt_s, pt_r, cb_s, cb_r, ui_s, ui_r, ut_s, ut_r, fi_s, fi_r, ft_s, ft_r, fo_s, fp_s,
 ):
     z, y, x, k = place()
     p0 = y * 4 + x
@@ -447,6 +447,47 @@
 
         each(0, 8, pass_on)
 
+    block = jnp.where(k == 0, z, 8)
+    zd = jnp.where(k == 0, zt, z)
+
+    def ft(t):
+        to = device(zd, rem(y + 2 + div(t, 2), 4), 2 * h + rem(t, 2), k)
+        return push(CX, FT.at[block], ft_s.at[t], ft_r.at[block], to)
+
+    def ft_here(t):
+        return (zd == z) & (div(t, 2) == 2) & (rem(t, 2) == rem(x, 2))
+
+    def fi(t):
+        to = device(z, rem(y + 2 + div(t, 2), 4), k * 2 + rem(t, 2), k)
+        return push(CI, FI.at[p0], fi_s.at[t], fi_r.at[p0], to)
+
+    def fi_here(t):
+        return (div(t, 2) == 2) & (k * 2 + rem(t, 2) == x)
+
+    @pl.when(sums_text)
+    def _():
+        def add_text(q, acc):
+            @pl.when(q != p0)
+            def _():
+                push(VB.at[0], UT.at[q], ut_s.at[0], ut_r.at[q], sib).wait_recv()
+
+            return acc + UT[q, 0:U].astype(F32)
+
+        CX[0:U] = lax.fori_loop(0, 16, add_text, jnp.zeros((U, Q), F32)).astype(BF)
+
+        def send(t):
+            @pl.when(ft_here(t))
+            def _():
+                FT[block] = CX[...]
+
+            @pl.when(jnp.logical_not(ft_here(t)))
+            def _():
+                ft(t).start()
+
+        each(0, 8, send)
+
+    out[0:R] = dot_nt(half_image, WI[...])
+
     for copy in (*z_near.values(), *z_far.values(), *near_t.values(), *relay_t.values(), *half_t, *sum_t):
         copy.wait_send()
     for n in POS.values():
@@ -466,47 +507,6 @@
 
     each(1, 16, pi_sent)
 
-    block = jnp.where(k == 0, z, 8)
-    zd = jnp.where(k == 0, zt, z)
-
-    def ft(t):
-        to = device(zd, rem(y + 2 + div(t, 4), 4), 2 * h + rem(div(t, 2), 2), rem(t, 2))
-        return push(CX, FT.at[block], ft_s.at[t], ft_r.at[block], to)
-
-    def ft_here(t):
-        return (zd == z) & (div(t, 4) == 2) & (rem(div(t, 2), 2) == rem(x, 2)) & (rem(t, 2) == k)
-
-    def fi(t):
-        to = device(z, rem(y + 2 + div(t, 4), 4), k * 2 + rem(div(t, 2), 2), rem(t, 2))
-        return push(CI, FI.at[p0], fi_s.at[t], fi_r.at[p0], to)
-
-    def fi_here(t):
-        return (div(t, 4) == 2) & (k * 2 + rem(div(t, 2), 2) == x) & (rem(t, 2) == k)
-
-    @pl.when(sums_text)
-    def _():
-        def add_text(q, acc):
-            @pl.when(q != p0)
-            def _():
-                push(VB.at[0], UT.at[q], ut_s.at[0], ut_r.at[q], sib).wait_recv()
-
-            return acc + UT[q, 0:U].astype(F32)
-
-        CX[0:U] = lax.fori_loop(0, 16, add_text, jnp.zeros((U, Q), F32)).astype(BF)
-
-        def send(t):
-            @pl.when(ft_here(t))
-            def _():
-                FT[block] = CX[...]
-
-            @pl.when(jnp.logical_not(ft_here(t)))
-            def _():
-                ft(t).start()
-
-        each(0, 16, send)
-
-    out[0:R] = dot_nt(half_image, WI[...])
-
     @pl.when(sums_image)
     def _():
         def add_image(d, acc):
@@ -524,18 +524,45 @@
             def _():
                 fi(t).start()
 
-        each(0, 16, send)
+        each(0, 8, send)
+
+    def ft_on(j):
+        return push(FT.at[j], FT.at[j], fp_s.at[j], ft_r.at[j], sib)
+
+    def fi_on(j):
+        return push(FI.at[j], FI.at[j], fo_s.at[j], fi_r.at[j], sib)
+
+    def ft_wait(j):
+        mine_j = ((k == 1) & (m == z)) if j == 8 else ((k == 0) & (z == j) & (zt == z))
+
+        @pl.when(jnp.logical_not(mine_j))
+        def _():
+            push(CX, FT.at[j], ft_s.at[0], ft_r.at[j], sib).wait_recv()
 
     for j in range(NB):
-        lanes = slice(j * Q, (j + 1) * Q)
-
-        mine_j = ((k == 1) & (m == z)) if j == 8 else ((k == 0) & (z == j) & (zt == z))
-
-        @pl.when(jnp.logical_not(mine_j))
+
+        @pl.when(k == j // 8)
+        def _():
+            ft_wait(j)
+            ft_on(j).start()
+
+    @pl.when(k == h)
+    def _():
+        for j in range(NB):
+
+            @pl.when(p0 != j)
+            def _():
+                push(CI, FI.at[j], fi_s.at[0], fi_r.at[j], sib).wait_recv()
+
+            fi_on(j).start()
+
+    for j in range(NB):
+
+        @pl.when(k != j // 8)
         def _():
             push(CX, FT.at[j], ft_s.at[0], ft_r.at[j], sib).wait_recv()
 
-        out[2 * R + U :, lanes] = FT[j, 0:U].astype(F32)
+        out[2 * R + U :, j * Q : (j + 1) * Q] = FT[j, 0:U].astype(F32)
 
     def ut_sent(u):
         @pl.when(ut_used(u) & jnp.logical_not(ut_here(u)))
@@ -556,16 +583,15 @@
             def _():
                 push(CX, FT.at[0], ft_s.at[t], ft_r.at[0], sib).wait_send()
 
-        each(0, 16, sent)
+        each(0, 8, sent)
 
     for j in range(NB):
-        lanes = slice(j * Q, (j + 1) * Q)
-
-        @pl.when(jnp.logical_not((p0 == j) & (h == k)))
+
+        @pl.when(k != h)
         def _():
             push(CI, FI.at[j], fi_s.at[0], fi_r.at[j], sib).wait_recv()
 
-        out[2 * R : 2 * R + U, lanes] = FI[j, 0:U].astype(F32)
+        out[2 * R : 2 * R + U, j * Q : (j + 1) * Q] = FI[j, 0:U].astype(F32)
 
     @pl.when(sums_image)
     def _():
@@ -574,7 +600,18 @@
             def _():
                 push(CI, FI.at[0], fi_s.at[t], fi_r.at[0], sib).wait_send()
 
-        each(0, 16, sent)
+        each(0, 8, sent)
+
+    for j in range(NB):
+
+        @pl.when(k == j // 8)
+        def _():
+            ft_on(j).wait_send()
+
+    @pl.when(k == h)
+    def _():
+        for j in range(NB):
+            fi_on(j).wait_send()
 
 
 def body(image_features, text_features, image_weight, text_weight, log_scale, bias):
@@ -600,7 +637,7 @@
             dma((4,)), dma((8,)), dma((8,)), dma((12,)), dma((12,)), *[dma((4,)) for _ in range(8)],
             dma((2,)), dma((2,)), dma((2,)), dma((2,)), dma((2,)), dma((2,)), dma((4,)), dma((4,)), *[dma((4,)) for _ in range(12)],
             dma((16,)), dma((16,)), dma((16,)), dma((16,)), dma((1,)), dma((1,)), dma((8,)), dma((8,)),
-            dma((16,)), dma((16,)), dma((16,)), dma((NB,)), dma((16,)), dma((NB,)),
+            dma((16,)), dma((16,)), dma((8,)), dma((NB,)), dma((8,)), dma((NB,)), dma((NB,)), dma((NB,)),
         ],
         compiler_params=pltpu.CompilerParams(
             collective_id=0, has_side_effects=True, vmem_limit_bytes=52 * 1024 * 1024

time: 67.4 us -> 66.4 us (0.985)
  Pallas kernels: 63.7 us -> 62.8 us
    pallas_call x1, Pallas kernels: 63.7 us -> 62.8 us  [body(): pl.pallas_call(kernel, out_shape=jax.ShapeDtypeStruct((2 * R + 2 * U, W),...]
where the time goes in v5:
time: 66.4 us
  Pallas kernels  62.8 us (95%)
  between operations  1.93 us (3%)
  local copies, waits for them, and re-layouts  1.61 us (2%)
    pallas_call x1, Pallas kernels, body(): pl.pallas_call(kernel, out_shape=jax.ShapeDtypeStruct((2 * R + 2 * U, W),...  62.8 us

profile of v5, /device:TPU:1, one launch (start us, length us, event | category | flops | bytes accessed | tf_op | source)
XLA Modules:
  0.0 66.4 jit_solution(8346216561291029309)
XLA Ops:
  1.9 62.8 %shard_map.93 = f32[208,1152]{1,0:T(8,128)S(1)} custom-call(bf16[32,1152]{1,0:T(8,128)(2,1)} %xi.1, bf16[32,1152]{1,0:T(8,128)(2,1)} %xt.1, bf16[1152,1152]{1,0:T(8,128)(2,1)} %wi_hbm.1, bf16[1152,1152]{1,0:T(8,128)(2,1)} %wt_hbm.1, f32[1,1]{1,0:T(1,128)} %bitcast.2.ls, f32[1,1]{1,0:T(1,128)} %bitcast.3.bs), custom_call_target="tpu_custom_call" | custom-call | tf_op jit(solution)/shard_map/pallas_call | solution.py:622
  64.7 0.9 %fusion = (f32[72,1152]{1,0:T(8,128)}, f32[72,1152]{1,0:T(8,128)}) fusion(f32[208,1152]{1,0:T(8,128)S(1)} %shard_map.93), kind=kLoop, calls=%fused_computation | loop fusion | bytes 1327104 | tf_op jit(solution)/shard_map/slice | solution.py:650
  65.6 0.7 %fusion.1 = (f32[32,1152]{1,0:T(8,128)}, f32[32,1152]{1,0:T(8,128)}) fusion(f32[208,1152]{1,0:T(8,128)S(1)} %shard_map.93), kind=kLoop, calls=%fused_computation.1 | loop fusion | bytes 589824 | tf_op jit(solution)/shard_map/slice | solution.py:650

commit v6 on v5

--- a/solution.py
+++ b/solution.py
@@ -91,13 +91,12 @@
         pltpu.make_async_copy(src, dst, lsem.at[n])
         for n, (src, dst) in enumerate(((xt, XT.at[OWN]), (xi, XI.at[0, 0]), (wt_hbm, WT), (wi_hbm, WI)))
     ]
+    bar = pltpu.get_barrier_semaphore()
+    near = [at_z(2), at_z(-2), at_x(2), at_y(2)] + [at(d) for at in (at_z, at_x, at_y) for d in (1, -1)] + [sib]
+    for to in near:
+        pl.semaphore_signal(bar, inc=1, device_id=to, device_id_type=MESH)
     for load in loads:
         load.start()
-
-    bar = pltpu.get_barrier_semaphore()
-    near = [at_z(d) for d in (1, -1, 2, -2)] + [at_x(d) for d in (1, 2, 3)] + [at_y(d) for d in (1, 2, 3)] + [sib]
-    for to in near:
-        pl.semaphore_signal(bar, inc=1, device_id=to, device_id_type=MESH)
 
     pad = jnp.zeros((8, UP - U, Q), BF)
     for buf in (SB, UB, VB.at[0:8], VB.at[8:16]):

time: 66.4 us -> 66.4 us (level)
  no operation moved by 1% of the time
where the time goes in v6:
time: 66.4 us; the launch traced here: 66.3 us
  Pallas kernels  62.7 us (94%)
  between operations  1.93 us (3%)
  local copies, waits for them, and re-layouts  1.61 us (2%)
    pallas_call x1, Pallas kernels, body(): pl.pallas_call(kernel, out_shape=jax.ShapeDtypeStruct((2 * R + 2 * U, W),...  62.7 us

profile of v6, /device:TPU:1, one launch (start us, length us, event | category | flops | bytes accessed | tf_op | source)
XLA Modules:
  0.0 66.3 jit_solution(12939605537207575963)
XLA Ops:
  1.9 62.7 %shard_map.93 = f32[208,1152]{1,0:T(8,128)S(1)} custom-call(bf16[32,1152]{1,0:T(8,128)(2,1)} %xi.1, bf16[32,1152]{1,0:T(8,128)(2,1)} %xt.1, bf16[1152,1152]{1,0:T(8,128)(2,1)} %wi_hbm.1, bf16[1152,1152]{1,0:T(8,128)(2,1)} %wt_hbm.1, f32[1,1]{1,0:T(1,128)} %bitcast.2.ls, f32[1,1]{1,0:T(1,128)} %bitcast.3.bs), custom_call_target="tpu_custom_call" | custom-call | tf_op jit(solution)/shard_map/pallas_call | solution.py:621
  64.7 0.9 %fusion = (f32[72,1152]{1,0:T(8,128)}, f32[72,1152]{1,0:T(8,128)}) fusion(f32[208,1152]{1,0:T(8,128)S(1)} %shard_map.93), kind=kLoop, calls=%fused_computation | loop fusion | bytes 1327104 | tf_op jit(solution)/shard_map/slice | solution.py:649
  65.5 0.7 %fusion.1 = (f32[32,1152]{1,0:T(8,128)}, f32[32,1152]{1,0:T(8,128)}) fusion(f32[208,1152]{1,0:T(8,128)S(1)} %shard_map.93), kind=kLoop, calls=%fused_computation.1 | loop fusion | bytes 589824 | tf_op jit(solution)/shard_map/slice | solution.py:649
